TPU v7x, 256 devices: a whole 4x4x8 slice. The times are simulated.
256 devices in a mesh: lat: 16 (over z, x_lo), lon: 16 (over y, x_hi, core).
Axes of the slice: x: 4 (x_hi: 2, x_lo: 2; x = x_hi * 2 + x_lo), y: 4, z: 8, core: 2. Of those that a mesh axis runs over, the one named last changes fastest.
Arguments:
- anomalies: bfloat16 [32, 64, 64, 256], P('lat', 'lon'), may hold values from -6 to 6
- innovations: bfloat16 [32, 64, 64, 256], P('lat', 'lon'), may hold values from -1.1953125 to 1.1953125
- taper_table: bfloat16 [16, 256, 256], replicated, may hold values from 0 to 1, as said below
- pair_own: int32 [16, 16, 200], P('lat', 'lon'), may hold values from 0 to 7, as said below
- pair_window: int32 [16, 16, 200], P('lat', 'lon'), may hold values from 0 to 47, as said below
- pair_taper: int32 [16, 16, 200], P('lat', 'lon'), may hold values from 0 to 15, as said below
- pair_owner: int32 [16, 16, 200], P('lat', 'lon'), may hold values from 0 to 1, as said below
- pair_count: int32 [16, 16], P('lat', 'lon'), may hold values from 8 to 200, as said below
Outputs:
- inflated: float32 [32, 64, 64, 256], P('lat', 'lon')
Inputs may be any that keep to these rules, and one draw needn't show every extreme that they name: Slots 0 to pair_count - 1 of a device are live; the later slots hold zeros in every pair list. Some device is full in every draw. `pair_own`: A live slot names each of the device's blocks as own block. `pair_window`: A live slot never names a window block beyond the poles, and each (own block, window block) pair stands once. `pair_owner`: for every live slot (a, b) other than a diagonal one (b the window position of a itself), the device of b holds a live mirror slot (b, a); the owner values of a slot and its mirror sum to one; a diagonal slot has owner 1 and no mirror. `pair_taper`: A mirror slot's taper index is its slot's index plus 8, modulo 2 * 8. `taper_table`: entry k + 8 is the transpose of entry k.
All inputs are finite; a program needn't handle non-finite values.
Results may differ from a plain program's by a relative error of at most 0.0033.
Values may be sent and summed in bfloat16 or wider, within the bound.
No kernel may reach another device: no remote copies, remote signals or barrier semaphores. Data moves between devices by JAX's collectives and lax.ppermute only.
A program may use at most 64 MiB of HBM per device.

v0:
```python
import jax
import jax.numpy as jnp
from jax import lax
from jax.sharding import PartitionSpec as P

MEMBERS = 64
BLOCK = 256
REACH = 2
GROUP = 8


def padded(array, sides, width):
    for axis, dim in sides:
        size, length = (lax.axis_size(axis), array.shape[dim])
        up = [(i, (i + 1) % size) for i in range(size)]
        down = [(j, i) for i, j in up]
        last = lax.slice_in_dim(array, length - width, length, axis=dim)
        leading = lax.slice_in_dim(array, 0, width, axis=dim)
        before = lax.ppermute(last, axis, up)
        after = lax.ppermute(leading, axis, down)
        array = jnp.concatenate([before, array, after], axis=dim)
    return array


def passed_along(value, axis, steps):
    count = lax.axis_size(axis)
    pairs = [(source, (source + steps) % count) for source in range(count)]
    return lax.ppermute(value, axis, pairs)


def from_behind(array, axis, by):
    size = lax.axis_size(axis)
    pairs = [(i, i + by) for i in range(size) if 0 <= i + by < size]
    return lax.ppermute(array, axis, pairs)


def one_hot(indices, count, dtype):
    return (indices[:, None] == jnp.arange(count, dtype=jnp.int32)[None, :]).astype(dtype)


def select_blocks(indices, table):
    picker = one_hot(indices, table.shape[0], jnp.bfloat16)
    picked = jnp.einsum("gn,nxy->gxy", picker, table, preferred_element_type=jnp.float32)
    return picked.astype(jnp.bfloat16)


def place_blocks(indices, weights, count, values):
    placer = one_hot(indices, count, jnp.float32) * weights[:, None]
    return jnp.einsum("gn,gmx->nmx", placer, values, precision=lax.Precision.HIGHEST)


def tile_group(
    home_anom, window_anom, window_innov, taper_table, home_part, window_part, taper_part
):
    anom_home = select_blocks(home_part, home_anom)
    anom_window = select_blocks(window_part, window_anom)
    product = jnp.einsum("gkx,gky->gxy", anom_home, anom_window, preferred_element_type=jnp.float32)
    tapers = select_blocks(taper_part, taper_table)
    covariance = (product / (MEMBERS - 1) * tapers).astype(jnp.bfloat16)
    innov_window = select_blocks(window_part, window_innov)
    to_home = jnp.einsum(
        "gmy,gxy->gmx", innov_window, covariance, preferred_element_type=jnp.float32
    )
    return (covariance, to_home)


def local(
    anomalies, innovations, taper_table, pair_own, pair_window, pair_taper, pair_owner, pair_count
):
    bands_dev = anomalies.shape[0]
    lons_dev = anomalies.shape[1]
    win_lat = bands_dev + 2 * REACH
    win_lon = lons_dev + 2 * REACH
    home_count = bands_dev * lons_dev
    window_count = win_lat * win_lon
    stacked = jnp.concatenate([anomalies, innovations], axis=2)
    window = padded(stacked, (("lat", 0), ("lon", 1)), REACH)
    window = window.reshape(window_count, 2 * MEMBERS, BLOCK)
    window_anom = window[:, :MEMBERS]
    window_innov = window[:, MEMBERS:]
    home_anom = anomalies.reshape(home_count, MEMBERS, BLOCK)
    home_innov = innovations.reshape(home_count, MEMBERS, BLOCK)
    home_index = pair_own.reshape(-1)
    window_index = pair_window.reshape(-1)
    taper_index = pair_taper.reshape(-1)
    owner_flag = pair_owner.reshape(-1)
    slot_total = home_index.shape[0]
    live_count = pair_count.reshape(())
    slot_iota = jnp.arange(slot_total, dtype=jnp.int32)
    group_iota = jnp.arange(GROUP, dtype=jnp.int32)
    wanted = (slot_iota < live_count) & (owner_flag == 1)
    ordering = jnp.argsort(jnp.where(wanted, 0, slot_total).astype(jnp.int32) + slot_iota)
    home_index = home_index[ordering]
    window_index = window_index[ordering]
    taper_index = taper_index[ordering]
    wanted_total = jnp.sum(wanted.astype(jnp.int32))
    group_trips = (wanted_total + GROUP - 1) // GROUP

    def one_group(group_step, partial_value):
        first_slot = group_step * GROUP
        home_part = lax.dynamic_slice_in_dim(home_index, first_slot, GROUP)
        window_part = lax.dynamic_slice_in_dim(window_index, first_slot, GROUP)
        taper_part = lax.dynamic_slice_in_dim(taper_index, first_slot, GROUP)
        weight = (first_slot + group_iota < wanted_total).astype(jnp.float32)
        covariance, to_home = tile_group(
            home_anom, window_anom, window_innov, taper_table, home_part, window_part, taper_part
        )
        innov_home = select_blocks(home_part, home_innov)
        to_window = jnp.einsum(
            "gmx,gxy->gmy", innov_home, covariance, preferred_element_type=jnp.float32
        )
        home_slot = (home_part // lons_dev + REACH) * win_lon + home_part % lons_dev + REACH
        diagonal = (home_slot == window_part).astype(jnp.float32)
        partial_value = partial_value + place_blocks(home_slot, weight, window_count, to_home)
        return partial_value + place_blocks(
            window_part, weight * (1.0 - diagonal), window_count, to_window
        )

    partial_value = lax.fori_loop(
        0, group_trips, one_group, jnp.zeros((window_count, MEMBERS, BLOCK), jnp.float32)
    )
    partial_value = partial_value.reshape(win_lat, win_lon, MEMBERS, BLOCK)
    from_west = passed_along(
        partial_value[:, REACH + lons_dev :].astype(jnp.bfloat16), "lon", 1
    ).astype(jnp.float32)
    from_east = passed_along(partial_value[:, :REACH].astype(jnp.bfloat16), "lon", -1).astype(
        jnp.float32
    )
    middle = partial_value[:, REACH : REACH + lons_dev]
    middle = middle.at[:, :REACH].add(from_west).at[:, lons_dev - REACH :].add(from_east)
    from_north = from_behind(middle[REACH + bands_dev :].astype(jnp.bfloat16), "lat", 1).astype(
        jnp.float32
    )
    from_south = from_behind(middle[:REACH].astype(jnp.bfloat16), "lat", -1).astype(jnp.float32)
    middle = (
        middle.at[REACH : 2 * REACH]
        .add(from_north)
        .at[bands_dev : bands_dev + REACH]
        .add(from_south)
    )
    increment = middle[REACH : REACH + bands_dev]
    prior = anomalies.astype(jnp.float32)
    posterior = prior - increment
    prior_spread = jnp.sqrt(jnp.sum(prior * prior, axis=2) / (MEMBERS - 1))
    posterior_spread = jnp.sqrt(jnp.sum(posterior * posterior, axis=2) / (MEMBERS - 1) + 1e-06)
    factor = 0.7 * prior_spread / posterior_spread + 0.3
    return posterior * factor[:, :, None, :]


def solution(mesh):
    placed = (
        P("lat", "lon", None, None),
        P("lat", "lon", None, None),
        P(),
        P("lat", "lon", None),
        P("lat", "lon", None),
        P("lat", "lon", None),
        P("lat", "lon", None),
        P("lat", "lon"),
    )
    return jax.shard_map(
        local, mesh=mesh, in_specs=placed, out_specs=P("lat", "lon", None, None), check_vma=False
    )
```

profile of v0, /device:TPU:225, one launch (start us, length us, event | category | flops | bytes accessed | tf_op | source)
XLA Modules:
  0.0 282.8 jit_solution(6591225670163361556)
XLA Ops:
  2.0 1.7 collective-permute-start.1
  3.7 22.4 %collective-permute-done.1 = bf16[2,4,128,256]{3,2,1,0:T(8,128)(2,1)S(1)} collective-permute-done((bf16[2,4,128,256]{3,2,1,0:T(8,128)(2,1)S(1)}, bf16[2,4,128,256]{3,2,1,0:T(8,128)(2,1)S(1)}, u32[]{:S(2)}, u32[]{:S(2)}) %collective-permute-start.1) | collective-permute-done | bytes 524320 | tf_op jit(solution)/shard_map/ppermute | solution.py:20
  26.9 1.3 fusion.51
  28.1 4.2 %collective-permute-start.2 = (bf16[6,2,128,256]{3,2,1,0:T(8,128)(2,1)}, bf16[6,2,128,256]{3,2,1,0:T(8,128)(2,1)}, u32[]{:S(2)}, u32[]{:S(2)}) collective-permute-start(bf16[6,2,128,256]{3,2,1,0:T(8,128)(2,1)} %get-tuple-element.308), channel_id=1, source_target_pairs={{0,1},{1,2},{2,3},{3,4},{4,5},{5,6},{6,7},{7,8},{8,9},{9,10},{10,1... | collective-permute-start | bytes 2359304 | tf_op jit(solution)/shard_map/ppermute | solution.py:19
  34.2 3.2 %sort.17 = (s32[200]{0:T(256)}, s32[200]{0:T(256)S(1)}) sort(s32[200]{0:T(256)S(1)} %get-tuple-element.312, s32[200]{0:T(256)S(1)} %iota.39), dimensions={0}, to_apply=%region_1.2 | sort | flops 1600 | bytes 3200 | tf_op jit(solution)/shard_map/jit(argsort)/sort | solution.py:92
  37.5 1.9 gather_fusion.2
  39.4 1.9 gather_fusion.1
  41.4 1.9 gather_fusion
  43.4 2.5 copy.13
  47.0 4.7 %collective-permute-done.3 = bf16[6,2,128,256]{3,2,1,0:T(8,128)(2,1)} collective-permute-done((bf16[6,2,128,256]{3,2,1,0:T(8,128)(2,1)}, bf16[6,2,128,256]{3,2,1,0:T(8,128)(2,1)}, u32[]{:S(2)}, u32[]{:S(2)}) %collective-permute-start.3) | collective-permute-done | bytes 786464 | tf_op jit(solution)/shard_map/ppermute | solution.py:20
  51.7 1.7 pad_maximum_fusion
  53.4 2.0 fusion.49
  56.4 194.3 %while.17 = (s32[]{:T(128)}, f32[48,64,256]{2,0,1:T(8,128)S(1)}, s32[]{:T(128)}, s32[200]{0:T(256)S(1)}, s32[]{:T(128)}, /*index=5*/s32[200]{0:T(256)S(1)}, bf16...) while((s32[]{:T(128)}, f32[48,64,256]{2,0,1:T(8,128)S(1)}, ...), condition=%wide.region_3.4_spmd.clone, body=%wide.region_2.3_spmd.clone.sunk | while | flops 402131712 | bytes 42468176 | solution.py:119
  57.8 1.2 fusion.102
  59.4 2.5 fusion.99
  64.6 2.8 fusion.101
  67.3 4.0 %add_add_fusion.2 = f32[48,64,256]{2,0,1:T(8,128)S(1)} fusion(f32[48,64,256]{2,0,1:T(8,128)S(1)} %get-tuple-element.413, f32[48,64,256]{2,0,1:T(8,128)S(1)} %fusion.101, f32[8,64,256]{2,1,0:T(8,128)S(1)} %fusion.103, f32[8]{0:T(128)S(1)} %get-tuple-element.395, s32[8]{0:T(128)S(1)} %get-tuple-element.393), kind=kOutput, calls=%fused_computation.4.clone.1 | convolution fusion | flops 77071104 | bytes 9961536 | tf_op jit(solution)/shard_map/while/body/gn,gmx->nmx/dot_general | solution.py:49
  74.3 2.5 fusion.99
  79.5 2.8 fusion.101
  82.3 4.0 %add_add_fusion.2 = f32[48,64,256]{2,0,1:T(8,128)S(1)} fusion(f32[48,64,256]{2,0,1:T(8,128)S(1)} %get-tuple-element.413, f32[48,64,256]{2,0,1:T(8,128)S(1)} %fusion.101, f32[8,64,256]{2,1,0:T(8,128)S(1)} %fusion.103, f32[8]{0:T(128)S(1)} %get-tuple-element.395, s32[8]{0:T(128)S(1)} %get-tuple-element.393), kind=kOutput, calls=%fused_computation.4.clone.1 | convolution fusion | flops 77071104 | bytes 9961536 | tf_op jit(solution)/shard_map/while/body/gn,gmx->nmx/dot_general | solution.py:49
  89.3 2.5 fusion.99
  94.5 2.8 fusion.101
  97.2 4.0 %add_add_fusion.2 = f32[48,64,256]{2,0,1:T(8,128)S(1)} fusion(f32[48,64,256]{2,0,1:T(8,128)S(1)} %get-tuple-element.413, f32[48,64,256]{2,0,1:T(8,128)S(1)} %fusion.101, f32[8,64,256]{2,1,0:T(8,128)S(1)} %fusion.103, f32[8]{0:T(128)S(1)} %get-tuple-element.395, s32[8]{0:T(128)S(1)} %get-tuple-element.393), kind=kOutput, calls=%fused_computation.4.clone.1 | convolution fusion | flops 77071104 | bytes 9961536 | tf_op jit(solution)/shard_map/while/body/gn,gmx->nmx/dot_general | solution.py:49
  102.7 1.2 fusion.102
  104.2 2.5 fusion.99
  109.4 2.8 fusion.101
  112.2 4.0 %add_add_fusion.2 = f32[48,64,256]{2,0,1:T(8,128)S(1)} fusion(f32[48,64,256]{2,0,1:T(8,128)S(1)} %get-tuple-element.413, f32[48,64,256]{2,0,1:T(8,128)S(1)} %fusion.101, f32[8,64,256]{2,1,0:T(8,128)S(1)} %fusion.103, f32[8]{0:T(128)S(1)} %get-tuple-element.395, s32[8]{0:T(128)S(1)} %get-tuple-element.393), kind=kOutput, calls=%fused_computation.4.clone.1 | convolution fusion | flops 77071104 | bytes 9961536 | tf_op jit(solution)/shard_map/while/body/gn,gmx->nmx/dot_general | solution.py:49
  119.2 2.5 fusion.99
  124.4 2.8 fusion.101
  127.1 4.0 %add_add_fusion.2 = f32[48,64,256]{2,0,1:T(8,128)S(1)} fusion(f32[48,64,256]{2,0,1:T(8,128)S(1)} %get-tuple-element.413, f32[48,64,256]{2,0,1:T(8,128)S(1)} %fusion.101, f32[8,64,256]{2,1,0:T(8,128)S(1)} %fusion.103, f32[8]{0:T(128)S(1)} %get-tuple-element.395, s32[8]{0:T(128)S(1)} %get-tuple-element.393), kind=kOutput, calls=%fused_computation.4.clone.1 | convolution fusion | flops 77071104 | bytes 9961536 | tf_op jit(solution)/shard_map/while/body/gn,gmx->nmx/dot_general | solution.py:49
  132.6 1.2 fusion.102
  134.1 2.5 fusion.99
  139.3 2.8 fusion.101
  142.1 4.0 %add_add_fusion.2 = f32[48,64,256]{2,0,1:T(8,128)S(1)} fusion(f32[48,64,256]{2,0,1:T(8,128)S(1)} %get-tuple-element.413, f32[48,64,256]{2,0,1:T(8,128)S(1)} %fusion.101, f32[8,64,256]{2,1,0:T(8,128)S(1)} %fusion.103, f32[8]{0:T(128)S(1)} %get-tuple-element.395, s32[8]{0:T(128)S(1)} %get-tuple-element.393), kind=kOutput, calls=%fused_computation.4.clone.1 | convolution fusion | flops 77071104 | bytes 9961536 | tf_op jit(solution)/shard_map/while/body/gn,gmx->nmx/dot_general | solution.py:49
  149.0 2.5 fusion.99
  154.3 2.8 fusion.101
  157.0 4.0 %add_add_fusion.2 = f32[48,64,256]{2,0,1:T(8,128)S(1)} fusion(f32[48,64,256]{2,0,1:T(8,128)S(1)} %get-tuple-element.413, f32[48,64,256]{2,0,1:T(8,128)S(1)} %fusion.101, f32[8,64,256]{2,1,0:T(8,128)S(1)} %fusion.103, f32[8]{0:T(128)S(1)} %get-tuple-element.395, s32[8]{0:T(128)S(1)} %get-tuple-element.393), kind=kOutput, calls=%fused_computation.4.clone.1 | convolution fusion | flops 77071104 | bytes 9961536 | tf_op jit(solution)/shard_map/while/body/gn,gmx->nmx/dot_general | solution.py:49
  162.4 1.2 fusion.102
  164.0 2.5 fusion.99
  169.2 2.8 fusion.101
  172.0 4.0 %add_add_fusion.2 = f32[48,64,256]{2,0,1:T(8,128)S(1)} fusion(f32[48,64,256]{2,0,1:T(8,128)S(1)} %get-tuple-element.413, f32[48,64,256]{2,0,1:T(8,128)S(1)} %fusion.101, f32[8,64,256]{2,1,0:T(8,128)S(1)} %fusion.103, f32[8]{0:T(128)S(1)} %get-tuple-element.395, s32[8]{0:T(128)S(1)} %get-tuple-element.393), kind=kOutput, calls=%fused_computation.4.clone.1 | convolution fusion | flops 77071104 | bytes 9961536 | tf_op jit(solution)/shard_map/while/body/gn,gmx->nmx/dot_general | solution.py:49
  177.4 1.2 fusion.102
  178.9 2.5 fusion.99
  184.1 2.8 fusion.101
  186.9 4.0 %add_add_fusion.2 = f32[48,64,256]{2,0,1:T(8,128)S(1)} fusion(f32[48,64,256]{2,0,1:T(8,128)S(1)} %get-tuple-element.413, f32[48,64,256]{2,0,1:T(8,128)S(1)} %fusion.101, f32[8,64,256]{2,1,0:T(8,128)S(1)} %fusion.103, f32[8]{0:T(128)S(1)} %get-tuple-element.395, s32[8]{0:T(128)S(1)} %get-tuple-element.393), kind=kOutput, calls=%fused_computation.4.clone.1 | convolution fusion | flops 77071104 | bytes 9961536 | tf_op jit(solution)/shard_map/while/body/gn,gmx->nmx/dot_general | solution.py:49
  193.9 2.5 fusion.99
  199.1 2.8 fusion.101
  201.9 4.0 %add_add_fusion.2 = f32[48,64,256]{2,0,1:T(8,128)S(1)} fusion(f32[48,64,256]{2,0,1:T(8,128)S(1)} %get-tuple-element.413, f32[48,64,256]{2,0,1:T(8,128)S(1)} %fusion.101, f32[8,64,256]{2,1,0:T(8,128)S(1)} %fusion.103, f32[8]{0:T(128)S(1)} %get-tuple-element.395, s32[8]{0:T(128)S(1)} %get-tuple-element.393), kind=kOutput, calls=%fused_computation.4.clone.1 | convolution fusion | flops 77071104 | bytes 9961536 | tf_op jit(solution)/shard_map/while/body/gn,gmx->nmx/dot_general | solution.py:49
  208.8 2.5 fusion.99
  214.0 2.8 fusion.101
  216.8 4.0 %add_add_fusion.2 = f32[48,64,256]{2,0,1:T(8,128)S(1)} fusion(f32[48,64,256]{2,0,1:T(8,128)S(1)} %get-tuple-element.413, f32[48,64,256]{2,0,1:T(8,128)S(1)} %fusion.101, f32[8,64,256]{2,1,0:T(8,128)S(1)} %fusion.103, f32[8]{0:T(128)S(1)} %get-tuple-element.395, s32[8]{0:T(128)S(1)} %get-tuple-element.393), kind=kOutput, calls=%fused_computation.4.clone.1 | convolution fusion | flops 77071104 | bytes 9961536 | tf_op jit(solution)/shard_map/while/body/gn,gmx->nmx/dot_general | solution.py:49
  223.8 2.5 fusion.99
  229.0 2.8 fusion.101
  231.8 4.0 %add_add_fusion.2 = f32[48,64,256]{2,0,1:T(8,128)S(1)} fusion(f32[48,64,256]{2,0,1:T(8,128)S(1)} %get-tuple-element.413, f32[48,64,256]{2,0,1:T(8,128)S(1)} %fusion.101, f32[8,64,256]{2,1,0:T(8,128)S(1)} %fusion.103, f32[8]{0:T(128)S(1)} %get-tuple-element.395, s32[8]{0:T(128)S(1)} %get-tuple-element.393), kind=kOutput, calls=%fused_computation.4.clone.1 | convolution fusion | flops 77071104 | bytes 9961536 | tf_op jit(solution)/shard_map/while/body/gn,gmx->nmx/dot_general | solution.py:49
  238.7 2.5 fusion.99
  243.9 2.8 fusion.101
  246.7 4.0 %add_add_fusion.2 = f32[48,64,256]{2,0,1:T(8,128)S(1)} fusion(f32[48,64,256]{2,0,1:T(8,128)S(1)} %get-tuple-element.413, f32[48,64,256]{2,0,1:T(8,128)S(1)} %fusion.101, f32[8,64,256]{2,1,0:T(8,128)S(1)} %fusion.103, f32[8]{0:T(128)S(1)} %get-tuple-element.395, s32[8]{0:T(128)S(1)} %get-tuple-element.393), kind=kOutput, calls=%fused_computation.4.clone.1 | convolution fusion | flops 77071104 | bytes 9961536 | tf_op jit(solution)/shard_map/while/body/gn,gmx->nmx/dot_general | solution.py:49
  250.7 1.8 copy.14
  253.6 4.1 %collective-permute-done.4 = bf16[6,2,64,256]{3,2,1,0:T(8,128)(2,1)S(1)} collective-permute-done((bf16[6,2,64,256]{3,2,1,0:T(8,128)(2,1)S(1)}, bf16[6,2,64,256]{3,2,1,0:T(8,128)(2,1)S(1)}, u32[]{:S(2)}, u32[]{:S(2)}) %collective-permute-start.4) | collective-permute-done | bytes 393248 | tf_op jit(solution)/shard_map/ppermute | solution.py:28
  257.7 7.3 %collective-permute-done.5 = bf16[6,2,64,256]{3,2,1,0:T(8,128)(2,1)S(1)} collective-permute-done((bf16[6,2,64,256]{3,2,1,0:T(8,128)(2,1)S(1)}, bf16[6,2,64,256]{3,2,1,0:T(8,128)(2,1)S(1)}, u32[]{:S(2)}, u32[]{:S(2)}) %collective-permute-start.5) | collective-permute-done | bytes 393248 | tf_op jit(solution)/shard_map/ppermute | solution.py:28
  265.4 1.9 collective-permute-start.6
  267.3 4.3 %collective-permute-start.7 = (bf16[2,4,64,256]{3,2,1,0:T(8,128)(2,1)S(1)}, bf16[2,4,64,256]{3,2,1,0:T(8,128)(2,1)S(1)}, u32[]{:S(2)}, u32[]{:S(2)}) collective-permute-start(bf16[2,4,64,256]{3,2,1,0:T(8,128)(2,1)S(1)} %get-tuple-element.311), channel_id=1, source_target_pairs={{16,0},{32,16},{48,32},{64,48},{80,64},{96,80},{112,96},{128,112},... | collective-permute-start | bytes 786440 | tf_op jit(solution)/shard_map/ppermute | solution.py:34
  271.5 4.3 %collective-permute-done.6 = bf16[2,4,64,256]{3,2,1,0:T(8,128)(2,1)S(1)} collective-permute-done((bf16[2,4,64,256]{3,2,1,0:T(8,128)(2,1)S(1)}, bf16[2,4,64,256]{3,2,1,0:T(8,128)(2,1)S(1)}, u32[]{:S(2)}, u32[]{:S(2)}) %collective-permute-start.6) | collective-permute-done | bytes 262176 | tf_op jit(solution)/shard_map/ppermute | solution.py:34
  275.9 5.8 %collective-permute-done.7 = bf16[2,4,64,256]{3,2,1,0:T(8,128)(2,1)S(1)} collective-permute-done((bf16[2,4,64,256]{3,2,1,0:T(8,128)(2,1)S(1)}, bf16[2,4,64,256]{3,2,1,0:T(8,128)(2,1)S(1)}, u32[]{:S(2)}, u32[]{:S(2)}) %collective-permute-start.7) | collective-permute-done | bytes 262176 | tf_op jit(solution)/shard_map/ppermute | solution.py:34
  (216 shorter events, 74.9 us)
Async XLA Ops:
  0.0 37.4 %copy-start = (s32[1,1,200]{2,1,0:T(1,128)S(1)}, s32[1,1,200]{2,1,0:T(1,128)}, u32[]{:S(2)}) copy-start(s32[1,1,200]{2,1,0:T(1,128)} %param.23) | copy-start | bytes 2404
  2.0 24.1 %collective-permute-start.1 = (bf16[2,4,128,256]{3,2,1,0:T(8,128)(2,1)S(1)}, bf16[2,4,128,256]{3,2,1,0:T(8,128)(2,1)S(1)}, u32[]{:S(2)}, u32[]{:S(2)}) collective-permute-start(bf16[2,4,128,256]{3,2,1,0:T(8,128)(2,1)S(1)} %constant_dynamic-update-slice_fusion), channel_id=1, source_target_pairs={{16,0},{32,16},{48,32},{64,48},{80,64},{96,80},{112,96},{128,112},... | collective-permute-start | bytes 1572872 | tf_op jit(solution)/shard_map/ppermute | solution.py:20
  3.7 22.4 %collective-permute-start = (bf16[2,4,128,256]{3,2,1,0:T(8,128)(2,1)S(1)}, bf16[2,4,128,256]{3,2,1,0:T(8,128)(2,1)S(1)}, u32[]{:S(2)}, u32[]{:S(2)}) collective-permute-start(bf16[2,4,128,256]{3,2,1,0:T(8,128)(2,1)S(1)} %constant_dynamic-update-slice_fusion), channel_id=1, source_target_pairs={{0,16},{16,32},{32,48},{48,64},{64,80},{80,96},{96,112},{112,128},... | collective-permute-start | bytes 1572872 | tf_op jit(solution)/shard_map/ppermute | solution.py:19
  26.1 0.8 copy-start.7
  26.9 6.1 %copy-start.8 = (s32[1,1,200]{2,1,0:T(1,128)S(1)}, s32[1,1,200]{2,1,0:T(1,128)}, u32[]{:S(2)}) copy-start(s32[1,1,200]{2,1,0:T(1,128)} %param.24) | copy-start | bytes 2404
  26.9 12.5 %copy-start.1 = (s32[1,1,200]{2,1,0:T(1,128)S(1)}, s32[1,1,200]{2,1,0:T(1,128)}, u32[]{:S(2)}) copy-start(s32[1,1,200]{2,1,0:T(1,128)} %param.22) | copy-start | bytes 2404
  26.9 14.5 %copy-start.2 = (s32[1,1,200]{2,1,0:T(1,128)S(1)}, s32[1,1,200]{2,1,0:T(1,128)}, u32[]{:S(2)}) copy-start(s32[1,1,200]{2,1,0:T(1,128)} %param.21) | copy-start | bytes 2404
  28.1 15.2 %copy-start.6 = (bf16[16,256,256]{2,1,0:T(8,128)(2,1)S(1)}, bf16[16,256,256]{2,1,0:T(8,128)(2,1)}, u32[]{:S(2)}) copy-start(bf16[16,256,256]{2,1,0:T(8,128)(2,1)} %param.20) | copy-start | bytes 6291460
  28.1 18.9 %collective-permute-start.2 = (bf16[6,2,128,256]{3,2,1,0:T(8,128)(2,1)}, bf16[6,2,128,256]{3,2,1,0:T(8,128)(2,1)}, u32[]{:S(2)}, u32[]{:S(2)}) collective-permute-start(bf16[6,2,128,256]{3,2,1,0:T(8,128)(2,1)} %get-tuple-element.308), channel_id=1, source_target_pairs={{0,1},{1,2},{2,3},{3,4},{4,5},{5,6},{6,7},{7,8},{8,9},{9,10},{10,1... | collective-permute-start | bytes 2359304 | tf_op jit(solution)/shard_map/ppermute | solution.py:19
  32.3 19.4 %collective-permute-start.3 = (bf16[6,2,128,256]{3,2,1,0:T(8,128)(2,1)}, bf16[6,2,128,256]{3,2,1,0:T(8,128)(2,1)}, u32[]{:S(2)}, u32[]{:S(2)}) collective-permute-start(bf16[6,2,128,256]{3,2,1,0:T(8,128)(2,1)} %get-tuple-element.309), channel_id=1, source_target_pairs={{1,0},{2,1},{3,2},{4,3},{5,4},{6,5},{7,6},{8,7},{9,8},{10,9},{11,1... | collective-permute-start | bytes 2359304 | tf_op jit(solution)/shard_map/ppermute | solution.py:20
  55.4 0.9 copy-start.5
  56.4 5.5 %copy-start.4 = (bf16[48,64,256]{2,1,0:T(8,128)(2,1)S(1)}, bf16[48,64,256]{2,1,0:T(8,128)(2,1)}, u32[]{:S(2)}) copy-start(bf16[48,64,256]{2,1,0:T(8,128)(2,1)} %get-tuple-element.436) | copy-start | bytes 4718596 | tf_op jit(solution)/shard_map/while
  59.1 3.8 %copy-start.3 = (bf16[16,256,256]{2,0,1:T(8,128)(2,1)S(1)}, bf16[16,256,256]{2,0,1:T(8,128)(2,1)}, u32[]{:S(2)}) copy-start(bf16[16,256,256]{2,0,1:T(8,128)(2,1)} %get-tuple-element.438) | copy-start | bytes 6291460 | tf_op jit(solution)/shard_map/while
  71.3 5.5 %copy-start.4 = (bf16[48,64,256]{2,1,0:T(8,128)(2,1)S(1)}, bf16[48,64,256]{2,1,0:T(8,128)(2,1)}, u32[]{:S(2)}) copy-start(bf16[48,64,256]{2,1,0:T(8,128)(2,1)} %get-tuple-element.436) | copy-start | bytes 4718596 | tf_op jit(solution)/shard_map/while
  74.0 3.8 %copy-start.3 = (bf16[16,256,256]{2,0,1:T(8,128)(2,1)S(1)}, bf16[16,256,256]{2,0,1:T(8,128)(2,1)}, u32[]{:S(2)}) copy-start(bf16[16,256,256]{2,0,1:T(8,128)(2,1)} %get-tuple-element.438) | copy-start | bytes 6291460 | tf_op jit(solution)/shard_map/while
  86.3 5.5 %copy-start.4 = (bf16[48,64,256]{2,1,0:T(8,128)(2,1)S(1)}, bf16[48,64,256]{2,1,0:T(8,128)(2,1)}, u32[]{:S(2)}) copy-start(bf16[48,64,256]{2,1,0:T(8,128)(2,1)} %get-tuple-element.436) | copy-start | bytes 4718596 | tf_op jit(solution)/shard_map/while
  89.0 3.8 %copy-start.3 = (bf16[16,256,256]{2,0,1:T(8,128)(2,1)S(1)}, bf16[16,256,256]{2,0,1:T(8,128)(2,1)}, u32[]{:S(2)}) copy-start(bf16[16,256,256]{2,0,1:T(8,128)(2,1)} %get-tuple-element.438) | copy-start | bytes 6291460 | tf_op jit(solution)/shard_map/while
  101.2 5.5 %copy-start.4 = (bf16[48,64,256]{2,1,0:T(8,128)(2,1)S(1)}, bf16[48,64,256]{2,1,0:T(8,128)(2,1)}, u32[]{:S(2)}) copy-start(bf16[48,64,256]{2,1,0:T(8,128)(2,1)} %get-tuple-element.436) | copy-start | bytes 4718596 | tf_op jit(solution)/shard_map/while
  103.9 3.8 %copy-start.3 = (bf16[16,256,256]{2,0,1:T(8,128)(2,1)S(1)}, bf16[16,256,256]{2,0,1:T(8,128)(2,1)}, u32[]{:S(2)}) copy-start(bf16[16,256,256]{2,0,1:T(8,128)(2,1)} %get-tuple-element.438) | copy-start | bytes 6291460 | tf_op jit(solution)/shard_map/while
  116.2 5.5 %copy-start.4 = (bf16[48,64,256]{2,1,0:T(8,128)(2,1)S(1)}, bf16[48,64,256]{2,1,0:T(8,128)(2,1)}, u32[]{:S(2)}) copy-start(bf16[48,64,256]{2,1,0:T(8,128)(2,1)} %get-tuple-element.436) | copy-start | bytes 4718596 | tf_op jit(solution)/shard_map/while
  118.9 3.8 %copy-start.3 = (bf16[16,256,256]{2,0,1:T(8,128)(2,1)S(1)}, bf16[16,256,256]{2,0,1:T(8,128)(2,1)}, u32[]{:S(2)}) copy-start(bf16[16,256,256]{2,0,1:T(8,128)(2,1)} %get-tuple-element.438) | copy-start | bytes 6291460 | tf_op jit(solution)/shard_map/while
  131.1 5.5 %copy-start.4 = (bf16[48,64,256]{2,1,0:T(8,128)(2,1)S(1)}, bf16[48,64,256]{2,1,0:T(8,128)(2,1)}, u32[]{:S(2)}) copy-start(bf16[48,64,256]{2,1,0:T(8,128)(2,1)} %get-tuple-element.436) | copy-start | bytes 4718596 | tf_op jit(solution)/shard_map/while
  133.8 3.8 %copy-start.3 = (bf16[16,256,256]{2,0,1:T(8,128)(2,1)S(1)}, bf16[16,256,256]{2,0,1:T(8,128)(2,1)}, u32[]{:S(2)}) copy-start(bf16[16,256,256]{2,0,1:T(8,128)(2,1)} %get-tuple-element.438) | copy-start | bytes 6291460 | tf_op jit(solution)/shard_map/while
  146.1 5.5 %copy-start.4 = (bf16[48,64,256]{2,1,0:T(8,128)(2,1)S(1)}, bf16[48,64,256]{2,1,0:T(8,128)(2,1)}, u32[]{:S(2)}) copy-start(bf16[48,64,256]{2,1,0:T(8,128)(2,1)} %get-tuple-element.436) | copy-start | bytes 4718596 | tf_op jit(solution)/shard_map/while
  148.7 3.8 %copy-start.3 = (bf16[16,256,256]{2,0,1:T(8,128)(2,1)S(1)}, bf16[16,256,256]{2,0,1:T(8,128)(2,1)}, u32[]{:S(2)}) copy-start(bf16[16,256,256]{2,0,1:T(8,128)(2,1)} %get-tuple-element.438) | copy-start | bytes 6291460 | tf_op jit(solution)/shard_map/while
  161.0 5.5 %copy-start.4 = (bf16[48,64,256]{2,1,0:T(8,128)(2,1)S(1)}, bf16[48,64,256]{2,1,0:T(8,128)(2,1)}, u32[]{:S(2)}) copy-start(bf16[48,64,256]{2,1,0:T(8,128)(2,1)} %get-tuple-element.436) | copy-start | bytes 4718596 | tf_op jit(solution)/shard_map/while
  163.7 3.8 %copy-start.3 = (bf16[16,256,256]{2,0,1:T(8,128)(2,1)S(1)}, bf16[16,256,256]{2,0,1:T(8,128)(2,1)}, u32[]{:S(2)}) copy-start(bf16[16,256,256]{2,0,1:T(8,128)(2,1)} %get-tuple-element.438) | copy-start | bytes 6291460 | tf_op jit(solution)/shard_map/while
  176.0 5.5 %copy-start.4 = (bf16[48,64,256]{2,1,0:T(8,128)(2,1)S(1)}, bf16[48,64,256]{2,1,0:T(8,128)(2,1)}, u32[]{:S(2)}) copy-start(bf16[48,64,256]{2,1,0:T(8,128)(2,1)} %get-tuple-element.436) | copy-start | bytes 4718596 | tf_op jit(solution)/shard_map/while
  178.6 3.8 %copy-start.3 = (bf16[16,256,256]{2,0,1:T(8,128)(2,1)S(1)}, bf16[16,256,256]{2,0,1:T(8,128)(2,1)}, u32[]{:S(2)}) copy-start(bf16[16,256,256]{2,0,1:T(8,128)(2,1)} %get-tuple-element.438) | copy-start | bytes 6291460 | tf_op jit(solution)/shard_map/while
  190.9 5.5 %copy-start.4 = (bf16[48,64,256]{2,1,0:T(8,128)(2,1)S(1)}, bf16[48,64,256]{2,1,0:T(8,128)(2,1)}, u32[]{:S(2)}) copy-start(bf16[48,64,256]{2,1,0:T(8,128)(2,1)} %get-tuple-element.436) | copy-start | bytes 4718596 | tf_op jit(solution)/shard_map/while
  193.6 3.8 %copy-start.3 = (bf16[16,256,256]{2,0,1:T(8,128)(2,1)S(1)}, bf16[16,256,256]{2,0,1:T(8,128)(2,1)}, u32[]{:S(2)}) copy-start(bf16[16,256,256]{2,0,1:T(8,128)(2,1)} %get-tuple-element.438) | copy-start | bytes 6291460 | tf_op jit(solution)/shard_map/while
  205.9 5.5 %copy-start.4 = (bf16[48,64,256]{2,1,0:T(8,128)(2,1)S(1)}, bf16[48,64,256]{2,1,0:T(8,128)(2,1)}, u32[]{:S(2)}) copy-start(bf16[48,64,256]{2,1,0:T(8,128)(2,1)} %get-tuple-element.436) | copy-start | bytes 4718596 | tf_op jit(solution)/shard_map/while
  208.5 3.8 %copy-start.3 = (bf16[16,256,256]{2,0,1:T(8,128)(2,1)S(1)}, bf16[16,256,256]{2,0,1:T(8,128)(2,1)}, u32[]{:S(2)}) copy-start(bf16[16,256,256]{2,0,1:T(8,128)(2,1)} %get-tuple-element.438) | copy-start | bytes 6291460 | tf_op jit(solution)/shard_map/while
  220.8 5.5 %copy-start.4 = (bf16[48,64,256]{2,1,0:T(8,128)(2,1)S(1)}, bf16[48,64,256]{2,1,0:T(8,128)(2,1)}, u32[]{:S(2)}) copy-start(bf16[48,64,256]{2,1,0:T(8,128)(2,1)} %get-tuple-element.436) | copy-start | bytes 4718596 | tf_op jit(solution)/shard_map/while
  223.5 3.8 %copy-start.3 = (bf16[16,256,256]{2,0,1:T(8,128)(2,1)S(1)}, bf16[16,256,256]{2,0,1:T(8,128)(2,1)}, u32[]{:S(2)}) copy-start(bf16[16,256,256]{2,0,1:T(8,128)(2,1)} %get-tuple-element.438) | copy-start | bytes 6291460 | tf_op jit(solution)/shard_map/while
  235.8 5.5 %copy-start.4 = (bf16[48,64,256]{2,1,0:T(8,128)(2,1)S(1)}, bf16[48,64,256]{2,1,0:T(8,128)(2,1)}, u32[]{:S(2)}) copy-start(bf16[48,64,256]{2,1,0:T(8,128)(2,1)} %get-tuple-element.436) | copy-start | bytes 4718596 | tf_op jit(solution)/shard_map/while
  238.4 3.8 %copy-start.3 = (bf16[16,256,256]{2,0,1:T(8,128)(2,1)S(1)}, bf16[16,256,256]{2,0,1:T(8,128)(2,1)}, u32[]{:S(2)}) copy-start(bf16[16,256,256]{2,0,1:T(8,128)(2,1)} %get-tuple-element.438) | copy-start | bytes 6291460 | tf_op jit(solution)/shard_map/while
  252.8 4.8 %collective-permute-start.4 = (bf16[6,2,64,256]{3,2,1,0:T(8,128)(2,1)S(1)}, bf16[6,2,64,256]{3,2,1,0:T(8,128)(2,1)S(1)}, u32[]{:S(2)}, u32[]{:S(2)}) collective-permute-start(bf16[6,2,64,256]{3,2,1,0:T(8,128)(2,1)S(1)} %get-tuple-element.307), channel_id=1, source_target_pairs={{0,1},{1,2},{2,3},{3,4},{4,5},{5,6},{6,7},{7,8},{8,9},{9,10},{10,1... | collective-permute-start | bytes 1179656 | tf_op jit(solution)/shard_map/ppermute | solution.py:28
  252.9 12.1 %collective-permute-start.5 = (bf16[6,2,64,256]{3,2,1,0:T(8,128)(2,1)S(1)}, bf16[6,2,64,256]{3,2,1,0:T(8,128)(2,1)S(1)}, u32[]{:S(2)}, u32[]{:S(2)}) collective-permute-start(bf16[6,2,64,256]{3,2,1,0:T(8,128)(2,1)S(1)} %get-tuple-element.306), channel_id=1, source_target_pairs={{0,15},{1,0},{2,1},{3,2},{4,3},{5,4},{6,5},{7,6},{8,7},{9,8},{10,9... | collective-permute-start | bytes 1179656 | tf_op jit(solution)/shard_map/ppermute | solution.py:28
  265.4 10.5 %collective-permute-start.6 = (bf16[2,4,64,256]{3,2,1,0:T(8,128)(2,1)S(1)}, bf16[2,4,64,256]{3,2,1,0:T(8,128)(2,1)S(1)}, u32[]{:S(2)}, u32[]{:S(2)}) collective-permute-start(bf16[2,4,64,256]{3,2,1,0:T(8,128)(2,1)S(1)} %get-tuple-element.310), channel_id=1, source_target_pairs={{0,16},{16,32},{32,48},{48,64},{64,80},{80,96},{96,112},{112,128},... | collective-permute-start | bytes 786440 | tf_op jit(solution)/shard_map/ppermute | solution.py:34
  267.3 14.4 %collective-permute-start.7 = (bf16[2,4,64,256]{3,2,1,0:T(8,128)(2,1)S(1)}, bf16[2,4,64,256]{3,2,1,0:T(8,128)(2,1)S(1)}, u32[]{:S(2)}, u32[]{:S(2)}) collective-permute-start(bf16[2,4,64,256]{3,2,1,0:T(8,128)(2,1)S(1)} %get-tuple-element.311), channel_id=1, source_target_pairs={{16,0},{32,16},{48,32},{64,48},{80,64},{96,80},{112,96},{128,112},... | collective-permute-start | bytes 786440 | tf_op jit(solution)/shard_map/ppermute | solution.py:34
where the time goes:
time: 284 us; the launch traced here: 283 us
  matrix products  175 us (62%)
  waiting for transfers between devices  49.6 us (17%)
  other arithmetic  24.9 us (9%)
  local copies, waits for them, and re-layouts  18.4 us (6%)
  starting transfers between devices  12.7 us (4%)
    dot_general x26, matrix products, place_blocks(): jnp.einsum('gn,gmx->nmx', placer, values, precision=lax.Precision.HIGHEST)  87.4 us
    dot_general x65, matrix products, select_blocks(): jnp.einsum('gn,nxy->gxy', picker, table, preferred_element_type=jnp.float32)  71 us
    ppermute x2, waiting for transfers between devices, padded(): after = lax.ppermute(leading, axis, down)  27 us
    ppermute x2, waiting for transfers between devices, passed_along(): return lax.ppermute(value, axis, pairs)  11.3 us
    ppermute x2, waiting for transfers between devices, from_behind(): return lax.ppermute(array, axis, pairs)  10.1 us
    convert_element_type x13, other arithmetic, one_group(): weight = (first_slot + group_iota < wanted_total).astype(jnp.float32)  8.81 us
    mul x13, other arithmetic, one_group(): weight * (1.0 - diagonal)  8.58 us
    dot_general x13, matrix products, tile_group(): jnp.einsum('gkx,gky->gxy', anom_home, anom_window, preferred_element_type...  6.82 us
  transfers between devices with their start and end apart: 8, of which 7 were waited for; matrix products, arithmetic and copies ran while one was open for 4% of the time, Pallas kernels for 0%

commit v1 on v0

v1 whole, which is shorter than its diff:
```python
import functools

import jax
import jax.numpy as jnp
from jax import lax
from jax.experimental import pallas as pl
from jax.experimental.pallas import tpu as pltpu
from jax.sharding import PartitionSpec as P

MEMBERS = 64
BLOCK = 256
REACH = 2
UNROLL = 16
LIST = 256
SLOTS = 200
COUNTS = 4 * LIST
VMEM_LIMIT = 24 * 2**20
F32 = jnp.float32
BF16 = jnp.bfloat16


def permuted(value, target):
    bands, lons = (lax.axis_size("lat"), lax.axis_size("lon"))
    pairs = []
    for i in range(bands):
        for j in range(lons):
            a, b = target(i, j)
            if 0 <= a < bands:
                pairs.append((i * lons + j, a * lons + b % lons))
    return lax.ppermute(value, ("lat", "lon"), pairs)


def to_partner(i, j):
    return (i ^ 1, j)


def to_beyond(i, j):
    return (i + 2 if i % 2 == 0 else i - 2, j)


def to_diagonal(i, j):
    return (i ^ 1, j + 1 if j % 2 else j - 1)


def to_other_core(i, j):
    return (i, j ^ 1)


def slot_entries(own, window, taper):
    row, lon = (window // 8, window % 8)
    odd_lat = lax.axis_index("lat") % 2
    odd_lon = lax.axis_index("lon") % 2
    partner_row = jnp.where(odd_lat == 1, 0, 2)
    rows = row // 2
    group = jnp.where(rows == 1, 0, jnp.where(rows == partner_row, 1, 2))
    west = lon < REACH
    east = lon >= 8 - REACH
    outer = jnp.where(odd_lon == 1, east, west)
    side = west | east
    center_slot = (row % 2) * 4 + lon - REACH
    side_slot = (row % 2) * 2 + jnp.where(west, lon, lon - 6)
    center_phase = group
    outer_phase = jnp.where(group == 1, 1, 2)
    outer_first = jnp.where(group == 0, 8, jnp.where(group == 1, 12, 16))
    inner_phase = group + 1
    inner_first = jnp.where(group == 0, 8, jnp.where(group == 1, 12, 0))
    phase = jnp.where(side, jnp.where(outer, outer_phase, inner_phase), center_phase)
    slot = jnp.where(
        side, jnp.where(outer, outer_first, inner_first) + side_slot, center_slot
    )
    return own + slot * 16 + taper * 1024 + phase * 16384


def pairs_of(lists, phase, home, window_anom, window_innov, tapers, total):
    def group(step, carry):
        for lane in range(UNROLL):
            entry = lists[phase * LIST + step * UNROLL + lane]
            own = entry & 15
            slot = (entry >> 4) & 63
            taper = (entry >> 10) & 15
            product = lax.dot_general(
                home[own & 7],
                window_anom[slot],
                (((0,), (0,)), ((), ())),
                preferred_element_type=F32,
            )
            tile = (product * tapers[taper].astype(F32)).astype(BF16)
            total[own] += lax.dot_general(
                tile, window_innov[slot], (((1,), (1,)), ((), ())), preferred_element_type=F32
            )
        return carry

    count = lists[COUNTS + phase]
    lax.fori_loop(0, (count + UNROLL - 1) // UNROLL, group, 0)


def first_kernel(entries, home, innov, tapers, total, lists):
    for phase in range(4):
        lists[COUNTS + phase] = 0

    def place(s, carry):
        entry = entries[s]
        phase = entry >> 14
        position = lists[COUNTS + phase]
        lists[phase * LIST + position] = entry & 16383
        lists[COUNTS + phase] = position + 1
        return carry

    lax.fori_loop(0, entries[SLOTS], place, 0)
    for phase in range(4):
        position = lists[COUNTS + phase]
        for lane in range(UNROLL):
            lists[phase * LIST + position + lane] = 8
    total[...] = jnp.zeros_like(total)
    pairs_of(lists, 0, home, home, innov, tapers, total)


def gathered(parts, sides, anom, innov):
    first = 0
    if parts is not None:
        anom[0:8] = parts[0][...]
        innov[0:8] = parts[1][...]
        first = 8
    for side in sides:
        anom[first : first + 4] = side[0]
        innov[first : first + 4] = side[1]
        first += 4


def middle_kernel(phase, lists, home, tapers, before, near_anom, near_innov, *rest):
    sides, (total, anom, innov) = (rest[:-3], rest[-3:])
    gathered((near_anom, near_innov), sides, anom, innov)
    total[...] = before[...]
    pairs_of(lists, phase, home, anom, innov, tapers, total)


def last_kernel(lists, home, tapers, before, side, out, total, anom, innov):
    gathered(None, (side,), anom, innov)
    total[...] = before[...]
    pairs_of(lists, 3, home, anom, innov, tapers, total)
    for own in range(8):
        prior = home[own].astype(F32)
        posterior = prior - total[own].T * (1.0 / (MEMBERS - 1))
        prior_spread = jnp.sqrt(jnp.sum(prior * prior, axis=0, keepdims=True) / (MEMBERS - 1))
        posterior_spread = jnp.sqrt(
            jnp.sum(posterior * posterior, axis=0, keepdims=True) / (MEMBERS - 1) + 1e-06
        )
        out[own] = posterior * (0.7 * prior_spread / posterior_spread + 0.3)


SMEM = pl.BlockSpec(memory_space=pltpu.SMEM)
VMEM = pl.BlockSpec(memory_space=pltpu.VMEM)
TOTAL = jax.ShapeDtypeStruct((9, BLOCK, MEMBERS), F32)


def called(kernel, name, specs, out_shape, out_specs, scratch, pairs):
    return pl.pallas_call(
        kernel,
        in_specs=specs,
        out_shape=out_shape,
        out_specs=out_specs,
        scratch_shapes=scratch,
        compiler_params=pltpu.CompilerParams(vmem_limit_bytes=VMEM_LIMIT),
        cost_estimate=pl.CostEstimate(
            flops=pairs * 8 * MEMBERS * BLOCK * BLOCK * 4, bytes_accessed=4 * 2**20, transcendentals=0
        ),
        name=name,
    )


def local(
    anomalies, innovations, taper_table, pair_own, pair_window, pair_taper, pair_owner, pair_count
):
    odd_lon = lax.axis_index("lon") % 2

    def outer(value):
        return jnp.where(odd_lon == 1, value[:, REACH:], value[:, :REACH])

    def inner(value):
        return jnp.where(odd_lon == 1, value[:, :REACH], value[:, REACH:])

    def both(part, first, second):
        return jnp.stack([part(first), part(second)])

    def flat(value):
        return value.reshape(8, MEMBERS, BLOCK)

    def flat_side(value):
        return value.reshape(2, 4, MEMBERS, BLOCK)

    partner = [permuted(v, to_partner) for v in (anomalies, innovations)]
    partner_outer = permuted(both(outer, anomalies, innovations), to_diagonal)
    home_inner = permuted(both(inner, anomalies, innovations), to_other_core)
    beyond = [permuted(v, to_beyond) for v in partner]
    home_outer = permuted(both(outer, *partner), to_diagonal)
    beyond_outer = permuted(partner_outer, to_beyond)
    partner_inner = permuted(both(inner, *partner), to_other_core)
    beyond_inner = permuted(both(inner, *beyond), to_other_core)

    entries = slot_entries(
        pair_own.reshape(-1), pair_window.reshape(-1), pair_taper.reshape(-1)
    )
    entries = jnp.concatenate([entries, pair_count.reshape(1), jnp.zeros((55,), jnp.int32)])
    home = flat(anomalies)
    scratch = lambda count: [pltpu.VMEM((count, MEMBERS, BLOCK), BF16)] * 2

    total, lists = called(
        first_kernel,
        "home_pairs",
        [SMEM, VMEM, VMEM, VMEM],
        (TOTAL, jax.ShapeDtypeStruct((COUNTS + 8,), jnp.int32)),
        (VMEM, SMEM),
        [],
        56,
    )(entries, home, flat(innovations), taper_table)
    total = called(
        functools.partial(middle_kernel, 1),
        "partner_pairs",
        [SMEM] + [VMEM] * 7,
        TOTAL,
        VMEM,
        scratch(16),
        63,
    )(
        lists,
        home,
        taper_table,
        total,
        flat(partner[0]),
        flat(partner[1]),
        flat_side(home_inner),
        flat_side(partner_outer),
    )
    total = called(
        functools.partial(middle_kernel, 2),
        "beyond_pairs",
        [SMEM] + [VMEM] * 8,
        TOTAL,
        VMEM,
        scratch(20),
        72,
    )(
        lists,
        home,
        taper_table,
        total,
        flat(beyond[0]),
        flat(beyond[1]),
        flat_side(home_outer),
        flat_side(partner_inner),
        flat_side(beyond_outer),
    )
    out = called(
        last_kernel,
        "inflation",
        [SMEM] + [VMEM] * 4,
        jax.ShapeDtypeStruct((8, MEMBERS, BLOCK), F32),
        VMEM,
        [pltpu.VMEM((9, BLOCK, MEMBERS), F32)] + scratch(4),
        9,
    )(lists, home, taper_table, total, flat_side(beyond_inner))
    return out.reshape(anomalies.shape)


def solution(mesh):
    placed = (
        P("lat", "lon", None, None),
        P("lat", "lon", None, None),
        P(),
        P("lat", "lon", None),
        P("lat", "lon", None),
        P("lat", "lon", None),
        P("lat", "lon", None),
        P("lat", "lon"),
    )
    return jax.shard_map(
        local, mesh=mesh, in_specs=placed, out_specs=P("lat", "lon", None, None), check_vma=False
    )
```

time: 284 us -> 54.4 us (0.19)
  matrix products: 175 us -> 0 us
  waiting for transfers between devices: 49.6 us -> 8.97 us
  Pallas kernels: 0 us -> 26 us
  other arithmetic: 24.9 us -> 2.31 us
  local copies, waits for them, and re-layouts: 18.4 us -> 1.62 us
    dot_general x130 -> x0, matrix products: 175 us -> none  [the longest x26 87.4 us: place_blocks(): jnp.einsum('gn,gmx->nmx', placer, values, precision=lax.Precision.HIGHEST)]
    ppermute x8 -> x10, waiting for transfers between devices: 49.6 us -> 8.97 us  [permuted(): return lax.ppermute(value, ('lat', 'lon'), pairs)]
    pallas_call x0 -> x4, Pallas kernels: none -> 26 us  [the longest x1 8.75 us: local(): called(first_kernel, 'home_pairs', [SMEM, VMEM, VMEM, VMEM], (TOTAL, jax....]
    mul x14 -> x1, other arithmetic: 9.5 us -> 0.01 us  [slot_entries(): return own + slot * 16 + taper * 1024 + phase * 16384]
    convert_element_type x13 -> x0, other arithmetic: 8.81 us -> none  [one_group(): weight = (first_slot + group_iota < wanted_total).astype(jnp.float32)]
    gather x3 -> x0, local copies, waits for them, and re-layouts: 5.85 us -> none  [the longest x1 1.95 us: local(): taper_index = taper_index[ordering]]
    slice x5 -> x0, local copies, waits for them, and re-layouts: 3.53 us -> none  [the longest x1 2.03 us: local(): window_anom = window[:, :MEMBERS]]
    sort x1 -> x0, other arithmetic: 3.19 us -> none  [local(): jnp.argsort(jnp.where(wanted, 0, slot_total).astype(jnp.int32) + slot_iota)]
  transfers between devices with their start and end apart: 8 -> 10, of which waited for: 7 -> 2; matrix products, arithmetic and copies ran while one was open for 4% -> 4% of each run, Pallas kernels for 0% -> 42%
where the time goes in v1:
time: 54.4 us; the launch traced here: 53.8 us
  Pallas kernels  26 us (48%)
  starting transfers between devices  14 us (26%)
  waiting for transfers between devices  8.97 us (16%)
  other arithmetic  2.31 us (4%)
  local copies, waits for them, and re-layouts  1.62 us (3%)
  between operations  0.89 us (2%)
    ppermute x10, starting transfers between devices, permuted(): return lax.ppermute(value, ('lat', 'lon'), pairs)  14 us
    ppermute x10, waiting for transfers between devices, permuted(): return lax.ppermute(value, ('lat', 'lon'), pairs)  8.97 us
    pallas_call x1, Pallas kernels, local(): called(first_kernel, 'home_pairs', [SMEM, VMEM, VMEM, VMEM], (TOTAL, jax....  8.75 us
    pallas_call x1, Pallas kernels, local(): called(functools.partial(middle_kernel, 2), 'beyond_pairs', [SMEM] + [VME...  7.73 us
    pallas_call x1, Pallas kernels, local(): called(functools.partial(middle_kernel, 1), 'partner_pairs', [SMEM] + [VM...  6.31 us
    pallas_call x1, Pallas kernels, local(): called(last_kernel, 'inflation', [SMEM] + [VMEM] * 4, jax.ShapeDtypeStruc...  3.24 us
    another operation x11, other arithmetic, both(): return jnp.stack([part(first), part(second)])  2.2 us
    unnamed x14, local copies, waits for them, and re-layouts  1.62 us
  transfers between devices with their start and end apart: 10, of which 2 were waited for; matrix products, arithmetic and copies ran while one was open for 4% of the time, Pallas kernels for 42%

profile of v1, /device:TPU:225, one launch (start us, length us, event | category | flops | bytes accessed | tf_op | source)
XLA Modules:
  0.0 53.8 jit_solution(15390697139427391369)
XLA Ops:
  0.0 0.0 copy-start.1
  0.0 0.0 copy-start
  0.0 0.0 copy-start.6
  0.0 0.0 copy-start.4
  0.0 0.0 copy-start.5
  0.0 1.3 %collective-permute-start = (bf16[2,4,64,256]{3,2,1,0:T(8,128)(2,1)}, bf16[2,4,64,256]{3,2,1,0:T(8,128)(2,1)S(1)}, u32[]{:S(2)}, u32[]{:S(2)}) collective-permute-start(bf16[2,4,64,256]{3,2,1,0:T(8,128)(2,1)} %param.8), channel_id=1, source_target_pairs={{0,16},{1,17},{2,18},{3,19},{4,20},{5,21},{6,22},{7,23},{8,24},{9,... | collective-permute-start | bytes 786440 | tf_op jit(solution)/shard_map/ppermute | solution.py:30
  1.3 0.3 collective-permute-start.1
  1.6 1.0 %select_bitcast_fusion.5 = (bf16[1,2,2,64,256]{4,3,2,1,0:T(8,128)(2,1)S(1)}, bf16[1,2,2,64,256]{4,3,2,1,0:T(8,128)(2,1)S(1)}) fusion(pred[]{:T(512)S(6)} %eq.22, bf16[2,4,64,256]{3,2,1,0:T(8,128)(2,1)} %param.8), kind=kLoop, calls=%fused_computation.14 | loop fusion | flops 131072 | bytes 524289 | tf_op jit(solution)/shard_map/stack | solution.py:183
  2.6 1.0 %select_bitcast_fusion.4 = (bf16[1,2,2,64,256]{4,3,2,1,0:T(8,128)(2,1)S(1)}, bf16[1,2,2,64,256]{4,3,2,1,0:T(8,128)(2,1)S(1)}) fusion(pred[]{:T(512)S(6)} %eq.22, bf16[2,4,64,256]{3,2,1,0:T(8,128)(2,1)} %param.9), kind=kLoop, calls=%fused_computation.13 | loop fusion | flops 131072 | bytes 524289 | tf_op jit(solution)/shard_map/stack | solution.py:183
  3.6 1.3 %collective-permute-start.2 = (bf16[2,2,2,64,256]{4,3,2,1,0:T(8,128)(2,1)S(1)}, bf16[2,2,2,64,256]{4,3,2,1,0:T(8,128)(2,1)S(1)}, u32[]{:S(2)}, u32[]{:S(2)}) collective-permute-start(bf16[2,2,2,64,256]{4,3,2,1,0:T(8,128)(2,1)S(1)} %pad_maximum_fusion), channel_id=1, source_target_pairs={{0,1},{1,0},{2,3},{3,2},{4,5},{5,4},{6,7},{7,6},{8,9},{9,8},{10,11... | collective-permute-start | bytes 786440 | tf_op jit(solution)/shard_map/ppermute | solution.py:30
  5.0 2.5 %collective-permute-start.3 = (bf16[2,2,2,64,256]{4,3,2,1,0:T(8,128)(2,1)S(1)}, bf16[2,2,2,64,256]{4,3,2,1,0:T(8,128)(2,1)S(1)}, u32[]{:S(2)}, u32[]{:S(2)}) collective-permute-start(bf16[2,2,2,64,256]{4,3,2,1,0:T(8,128)(2,1)S(1)} %pad_maximum_fusion.1), channel_id=1, source_target_pairs={{0,31},{1,18},{2,17},{3,20},{4,19},{5,22},{6,21},{7,24},{8,23},{9,... | collective-permute-start | bytes 786440 | tf_op jit(solution)/shard_map/ppermute | solution.py:30
  7.5 0.0 copy-done.6
  8.1 0.0 copy-done.4
  8.1 0.0 copy-done.5
  8.2 0.1 pad_add_fusion.entries
  8.3 0.0 copy-done.1
  8.3 0.0 copy-done
  8.3 0.0 copy-start.2
  8.3 1.6 %copy-done.2 = bf16[16,256,256]{2,1,0:T(8,128)(2,1)S(1)} copy-done((bf16[16,256,256]{2,1,0:T(8,128)(2,1)S(1)}, bf16[16,256,256]{2,1,0:T(8,128)(2,1)}, u32[]{:S(2)}) %copy-start.2) | copy-done | bytes 2097176
  9.9 8.8 %home_pairs.1 = (f32[9,256,64]{2,1,0:T(8,128)S(1)}, s32[1032]{0:T(1024)S(1)}) custom-call(s32[256]{0:T(256)S(1)} %pad_add_fusion.entries, bf16[8,64,256]{2,1,0:T(8,128)(2,1)S(1)} %bitcast.39, bf16[8,64,256]{2,1,0:T(8,128)(2,1)S(1)} %bitcast.38, bf16[16,256,256]{2,1,0:T(8,128)(2,1)S(1)} %copy-done.2), custom_call_target="tpu_custom_call" | custom-call | flops 7516192768 | bytes 4194304 | tf_op jit(solution)/shard_map/home_pairs/pallas_call | solution.py:207
  18.6 0.0 copy-start.3
  18.6 0.0 collective-permute-done
  18.7 0.0 collective-permute-done.1
  18.7 0.1 collective-permute-start.6
  18.9 3.0 %collective-permute-start.7 = (bf16[2,2,2,64,256]{4,3,2,1,0:T(8,128)(2,1)S(1)}, bf16[2,2,2,64,256]{4,3,2,1,0:T(8,128)(2,1)S(1)}, u32[]{:S(2)}, u32[]{:S(2)}) collective-permute-start(bf16[2,2,2,64,256]{4,3,2,1,0:T(8,128)(2,1)S(1)} %pad_maximum_fusion.3), channel_id=1, source_target_pairs={{0,1},{1,0},{2,3},{3,2},{4,5},{5,4},{6,7},{7,6},{8,9},{9,8},{10,11... | collective-permute-start | bytes 786440 | tf_op jit(solution)/shard_map/ppermute | solution.py:30
  21.9 1.3 %collective-permute-start.4 = (bf16[2,4,64,256]{3,2,1,0:T(8,128)(2,1)S(1)}, bf16[2,4,64,256]{3,2,1,0:T(8,128)(2,1)S(1)}, u32[]{:S(2)}, u32[]{:S(2)}) collective-permute-start(bf16[2,4,64,256]{3,2,1,0:T(8,128)(2,1)S(1)} %collective-permute-done), channel_id=1, source_target_pairs={{0,32},{1,33},{2,34},{3,35},{4,36},{5,37},{6,38},{7,39},{8,40},{9,... | collective-permute-start | bytes 786440 | tf_op jit(solution)/shard_map/ppermute | solution.py:30
  23.2 0.0 collective-permute-done.2
  23.2 1.3 %collective-permute-start.5 = (bf16[2,4,64,256]{3,2,1,0:T(8,128)(2,1)S(1)}, bf16[2,4,64,256]{3,2,1,0:T(8,128)(2,1)S(1)}, u32[]{:S(2)}, u32[]{:S(2)}) collective-permute-start(bf16[2,4,64,256]{3,2,1,0:T(8,128)(2,1)S(1)} %collective-permute-done.1), channel_id=1, source_target_pairs={{0,32},{1,33},{2,34},{3,35},{4,36},{5,37},{6,38},{7,39},{8,40},{9,... | collective-permute-start | bytes 786440 | tf_op jit(solution)/shard_map/ppermute | solution.py:30
  24.5 0.0 collective-permute-done.3
  24.5 0.0 copy-done.3
  24.5 6.3 %partner_pairs.1.before = f32[9,256,64]{2,1,0:T(8,128)S(1)} custom-call(s32[1032]{0:T(1024)S(1)} %get-tuple-element.7.lists, bf16[8,64,256]{2,1,0:T(8,128)(2,1)S(1)} %bitcast.40, bf16[16,256,256]{2,1,0:T(8,128)(2,1)S(1)} %copy-done.3, f32[9,256,64]{2,1,0:T(8,128)S(1)} %get-tuple-element.8.before, bf16[8,64,256]{2,1,0:T(8,128)(2,1)S(1)} %bitcast.43, ...), custom_call_target="tpu_custom_call" | custom-call | flops 8455716864 | bytes 4194304 | tf_op jit(solution)/shard_map/partner_pairs/pallas_call | solution.py:216
  30.8 1.3 %collective-permute-start.8 = (bf16[2,2,2,64,256]{4,3,2,1,0:T(8,128)(2,1)S(1)}, bf16[2,2,2,64,256]{4,3,2,1,0:T(8,128)(2,1)S(1)}, u32[]{:S(2)}, u32[]{:S(2)}) collective-permute-start(bf16[2,2,2,64,256]{4,3,2,1,0:T(8,128)(2,1)S(1)} %collective-permute-done.3), channel_id=1, source_target_pairs={{0,32},{1,33},{2,34},{3,35},{4,36},{5,37},{6,38},{7,39},{8,40},{9,... | collective-permute-start | bytes 786440 | tf_op jit(solution)/shard_map/ppermute | solution.py:30
  32.1 5.0 %collective-permute-done.5 = bf16[2,4,64,256]{3,2,1,0:T(8,128)(2,1)S(1)} collective-permute-done((bf16[2,4,64,256]{3,2,1,0:T(8,128)(2,1)S(1)}, bf16[2,4,64,256]{3,2,1,0:T(8,128)(2,1)S(1)}, u32[]{:S(2)}, u32[]{:S(2)}) %collective-permute-start.5) | collective-permute-done | bytes 262176 | tf_op jit(solution)/shard_map/ppermute | solution.py:30
  37.2 0.0 collective-permute-done.4
  37.3 1.6 %collective-permute-start.9 = (bf16[2,2,2,64,256]{4,3,2,1,0:T(8,128)(2,1)S(1)}, bf16[2,2,2,64,256]{4,3,2,1,0:T(8,128)(2,1)S(1)}, u32[]{:S(2)}, u32[]{:S(2)}) collective-permute-start(bf16[2,2,2,64,256]{4,3,2,1,0:T(8,128)(2,1)S(1)} %pad_maximum_fusion.4), channel_id=1, source_target_pairs={{0,1},{1,0},{2,3},{3,2},{4,5},{5,4},{6,7},{7,6},{8,9},{9,8},{10,11... | collective-permute-start | bytes 786440 | tf_op jit(solution)/shard_map/ppermute | solution.py:30
  38.9 0.0 collective-permute-done.6
  38.9 0.0 collective-permute-done.7
  38.9 3.9 %collective-permute-done.8 = bf16[2,2,2,64,256]{4,3,2,1,0:T(8,128)(2,1)S(1)} collective-permute-done((bf16[2,2,2,64,256]{4,3,2,1,0:T(8,128)(2,1)S(1)}, bf16[2,2,2,64,256]{4,3,2,1,0:T(8,128)(2,1)S(1)}, u32[]{:S(2)}, u32[]{:S(2)}) %collective-permute-start.8) | collective-permute-done | bytes 262176 | tf_op jit(solution)/shard_map/ppermute | solution.py:30
  42.8 7.7 %beyond_pairs.1.before = f32[9,256,64]{2,1,0:T(8,128)S(1)} custom-call(s32[1032]{0:T(1024)S(1)} %get-tuple-element.7.lists, bf16[8,64,256]{2,1,0:T(8,128)(2,1)S(1)} %bitcast.41, bf16[16,256,256]{2,1,0:T(8,128)(2,1)S(1)} %copy-done.3, f32[9,256,64]{2,1,0:T(8,128)S(1)} %partner_pairs.1.before, bf16[8,64,256]{2,1,0:T(8,128)(2,1)S(1)} %bitcast.45, ...), custom_call_target="tpu_custom_call" | custom-call | flops 9663676416 | bytes 4194304 | tf_op jit(solution)/shard_map/beyond_pairs/pallas_call | solution.py:234
  50.5 0.0 collective-permute-done.9
  50.5 3.2 %inflation.1 = f32[8,64,256]{2,1,0:T(8,128)} custom-call(s32[1032]{0:T(1024)S(1)} %get-tuple-element.7.lists, bf16[8,64,256]{2,1,0:T(8,128)(2,1)S(1)} %bitcast.42, bf16[16,256,256]{2,1,0:T(8,128)(2,1)S(1)} %copy-done.3, f32[9,256,64]{2,1,0:T(8,128)S(1)} %beyond_pairs.1.before, bf16[2,4,64,256]{3,2,1,0:T(8,128)(2,1)S(1)} %bitcast.52), custom_call_target="tpu_custom_call" | custom-call | flops 1207959552 | bytes 4194304 | tf_op jit(solution)/shard_map/inflation/pallas_call | solution.py:253
  (12 shorter events, 0.3 us)
Async XLA Ops:
  0.0 8.3 %copy-start.1 = (bf16[2,4,64,256]{3,2,1,0:T(8,128)(2,1)S(1)}, bf16[2,4,64,256]{3,2,1,0:T(8,128)(2,1)}, u32[]{:S(2)}) copy-start(bf16[2,4,64,256]{3,2,1,0:T(8,128)(2,1)} %param.8) | copy-start | bytes 786436
  0.0 8.3 %copy-start = (bf16[2,4,64,256]{3,2,1,0:T(8,128)(2,1)S(1)}, bf16[2,4,64,256]{3,2,1,0:T(8,128)(2,1)}, u32[]{:S(2)}) copy-start(bf16[2,4,64,256]{3,2,1,0:T(8,128)(2,1)} %param.9) | copy-start | bytes 786436
  0.0 7.5 %copy-start.6 = (s32[1,1,200]{2,1,0:T(1,128)S(1)}, s32[1,1,200]{2,1,0:T(1,128)}, u32[]{:S(2)}) copy-start(s32[1,1,200]{2,1,0:T(1,128)} %param.13) | copy-start | bytes 2404
  0.0 8.1 %copy-start.4 = (s32[1,1,200]{2,1,0:T(1,128)S(1)}, s32[1,1,200]{2,1,0:T(1,128)}, u32[]{:S(2)}) copy-start(s32[1,1,200]{2,1,0:T(1,128)} %param.11) | copy-start | bytes 2404
  0.0 8.1 %copy-start.5 = (s32[1,1,200]{2,1,0:T(1,128)S(1)}, s32[1,1,200]{2,1,0:T(1,128)}, u32[]{:S(2)}) copy-start(s32[1,1,200]{2,1,0:T(1,128)} %param.12) | copy-start | bytes 2404
  0.0 18.6 %collective-permute-start = (bf16[2,4,64,256]{3,2,1,0:T(8,128)(2,1)}, bf16[2,4,64,256]{3,2,1,0:T(8,128)(2,1)S(1)}, u32[]{:S(2)}, u32[]{:S(2)}) collective-permute-start(bf16[2,4,64,256]{3,2,1,0:T(8,128)(2,1)} %param.8), channel_id=1, source_target_pairs={{0,16},{1,17},{2,18},{3,19},{4,20},{5,21},{6,22},{7,23},{8,24},{9,... | collective-permute-start | bytes 786440 | tf_op jit(solution)/shard_map/ppermute | solution.py:30
  1.3 17.3 %collective-permute-start.1 = (bf16[2,4,64,256]{3,2,1,0:T(8,128)(2,1)}, bf16[2,4,64,256]{3,2,1,0:T(8,128)(2,1)S(1)}, u32[]{:S(2)}, u32[]{:S(2)}) collective-permute-start(bf16[2,4,64,256]{3,2,1,0:T(8,128)(2,1)} %param.9), channel_id=1, source_target_pairs={{0,16},{1,17},{2,18},{3,19},{4,20},{5,21},{6,22},{7,23},{8,24},{9,... | collective-permute-start | bytes 786440 | tf_op jit(solution)/shard_map/ppermute | solution.py:30
  3.6 19.6 %collective-permute-start.2 = (bf16[2,2,2,64,256]{4,3,2,1,0:T(8,128)(2,1)S(1)}, bf16[2,2,2,64,256]{4,3,2,1,0:T(8,128)(2,1)S(1)}, u32[]{:S(2)}, u32[]{:S(2)}) collective-permute-start(bf16[2,2,2,64,256]{4,3,2,1,0:T(8,128)(2,1)S(1)} %pad_maximum_fusion), channel_id=1, source_target_pairs={{0,1},{1,0},{2,3},{3,2},{4,5},{5,4},{6,7},{7,6},{8,9},{9,8},{10,11... | collective-permute-start | bytes 786440 | tf_op jit(solution)/shard_map/ppermute | solution.py:30
  5.0 19.5 %collective-permute-start.3 = (bf16[2,2,2,64,256]{4,3,2,1,0:T(8,128)(2,1)S(1)}, bf16[2,2,2,64,256]{4,3,2,1,0:T(8,128)(2,1)S(1)}, u32[]{:S(2)}, u32[]{:S(2)}) collective-permute-start(bf16[2,2,2,64,256]{4,3,2,1,0:T(8,128)(2,1)S(1)} %pad_maximum_fusion.1), channel_id=1, source_target_pairs={{0,31},{1,18},{2,17},{3,20},{4,19},{5,22},{6,21},{7,24},{8,23},{9,... | collective-permute-start | bytes 786440 | tf_op jit(solution)/shard_map/ppermute | solution.py:30
  8.3 1.6 %copy-start.2 = (bf16[16,256,256]{2,1,0:T(8,128)(2,1)S(1)}, bf16[16,256,256]{2,1,0:T(8,128)(2,1)}, u32[]{:S(2)}) copy-start(bf16[16,256,256]{2,1,0:T(8,128)(2,1)} %tapers.7) | copy-start | bytes 6291460
  18.6 5.9 %copy-start.3 = (bf16[16,256,256]{2,1,0:T(8,128)(2,1)S(1)}, bf16[16,256,256]{2,1,0:T(8,128)(2,1)}, u32[]{:S(2)}) copy-start(bf16[16,256,256]{2,1,0:T(8,128)(2,1)} %tapers.7) | copy-start | bytes 6291460
  18.7 20.1 %collective-permute-start.6 = (bf16[2,2,2,64,256]{4,3,2,1,0:T(8,128)(2,1)S(1)}, bf16[2,2,2,64,256]{4,3,2,1,0:T(8,128)(2,1)S(1)}, u32[]{:S(2)}, u32[]{:S(2)}) collective-permute-start(bf16[2,2,2,64,256]{4,3,2,1,0:T(8,128)(2,1)S(1)} %pad_maximum_fusion.2), channel_id=1, source_target_pairs={{0,31},{1,18},{2,17},{3,20},{4,19},{5,22},{6,21},{7,24},{8,23},{9,... | collective-permute-start | bytes 786440 | tf_op jit(solution)/shard_map/ppermute | solution.py:30
  18.9 20.0 %collective-permute-start.7 = (bf16[2,2,2,64,256]{4,3,2,1,0:T(8,128)(2,1)S(1)}, bf16[2,2,2,64,256]{4,3,2,1,0:T(8,128)(2,1)S(1)}, u32[]{:S(2)}, u32[]{:S(2)}) collective-permute-start(bf16[2,2,2,64,256]{4,3,2,1,0:T(8,128)(2,1)S(1)} %pad_maximum_fusion.3), channel_id=1, source_target_pairs={{0,1},{1,0},{2,3},{3,2},{4,5},{5,4},{6,7},{7,6},{8,9},{9,8},{10,11... | collective-permute-start | bytes 786440 | tf_op jit(solution)/shard_map/ppermute | solution.py:30
  21.9 15.3 %collective-permute-start.4 = (bf16[2,4,64,256]{3,2,1,0:T(8,128)(2,1)S(1)}, bf16[2,4,64,256]{3,2,1,0:T(8,128)(2,1)S(1)}, u32[]{:S(2)}, u32[]{:S(2)}) collective-permute-start(bf16[2,4,64,256]{3,2,1,0:T(8,128)(2,1)S(1)} %collective-permute-done), channel_id=1, source_target_pairs={{0,32},{1,33},{2,34},{3,35},{4,36},{5,37},{6,38},{7,39},{8,40},{9,... | collective-permute-start | bytes 786440 | tf_op jit(solution)/shard_map/ppermute | solution.py:30
  23.2 14.0 %collective-permute-start.5 = (bf16[2,4,64,256]{3,2,1,0:T(8,128)(2,1)S(1)}, bf16[2,4,64,256]{3,2,1,0:T(8,128)(2,1)S(1)}, u32[]{:S(2)}, u32[]{:S(2)}) collective-permute-start(bf16[2,4,64,256]{3,2,1,0:T(8,128)(2,1)S(1)} %collective-permute-done.1), channel_id=1, source_target_pairs={{0,32},{1,33},{2,34},{3,35},{4,36},{5,37},{6,38},{7,39},{8,40},{9,... | collective-permute-start | bytes 786440 | tf_op jit(solution)/shard_map/ppermute | solution.py:30
  30.8 11.9 %collective-permute-start.8 = (bf16[2,2,2,64,256]{4,3,2,1,0:T(8,128)(2,1)S(1)}, bf16[2,2,2,64,256]{4,3,2,1,0:T(8,128)(2,1)S(1)}, u32[]{:S(2)}, u32[]{:S(2)}) collective-permute-start(bf16[2,2,2,64,256]{4,3,2,1,0:T(8,128)(2,1)S(1)} %collective-permute-done.3), channel_id=1, source_target_pairs={{0,32},{1,33},{2,34},{3,35},{4,36},{5,37},{6,38},{7,39},{8,40},{9,... | collective-permute-start | bytes 786440 | tf_op jit(solution)/shard_map/ppermute | solution.py:30
  37.3 13.3 %collective-permute-start.9 = (bf16[2,2,2,64,256]{4,3,2,1,0:T(8,128)(2,1)S(1)}, bf16[2,2,2,64,256]{4,3,2,1,0:T(8,128)(2,1)S(1)}, u32[]{:S(2)}, u32[]{:S(2)}) collective-permute-start(bf16[2,2,2,64,256]{4,3,2,1,0:T(8,128)(2,1)S(1)} %pad_maximum_fusion.4), channel_id=1, source_target_pairs={{0,1},{1,0},{2,3},{3,2},{4,5},{5,4},{6,7},{7,6},{8,9},{9,8},{10,11... | collective-permute-start | bytes 786440 | tf_op jit(solution)/shard_map/ppermute | solution.py:30

commit v2 on v1

v2 whole, which is shorter than its diff:
```python
import functools

import jax
import jax.numpy as jnp
from jax import lax
from jax.experimental import pallas as pl
from jax.experimental.pallas import tpu as pltpu
from jax.sharding import PartitionSpec as P

MEMBERS = 64
BLOCK = 256
REACH = 2
UNROLL = 4
LIST = 264
SLOTS = 200
PHASES = 5
COUNTS = (PHASES + 1) * LIST
VMEM_LIMIT = 8 * 2**20
F32 = jnp.float32
BF16 = jnp.bfloat16


def permuted(value, target):
    bands, lons = (lax.axis_size("lat"), lax.axis_size("lon"))
    pairs = []
    for i in range(bands):
        for j in range(lons):
            a, b = target(i, j)
            pairs.append((i * lons + j, a * lons + b % lons))
    return lax.ppermute(value, ("lat", "lon"), pairs)


def to_partner(i, j):
    return (i ^ 1, j)


def to_beyond(i, j):
    last = lax.axis_size("lat") - 1
    target = i + 2 if i % 2 == 0 else i - 2
    return (target if 0 <= target <= last else i ^ 1, j)


def to_far_diagonal(i, j):
    last = lax.axis_size("lat") - 1
    target = i + 1 if i % 2 else i - 1
    return (target if 0 <= target <= last else i, j + 1 if j % 2 else j - 1)


def to_diagonal(i, j):
    return (i ^ 1, j + 1 if j % 2 else j - 1)


def to_other_core(i, j):
    return (i, j ^ 1)


def slot_entries(own, window, taper, count):
    row, lon = (window // 8, window % 8)
    odd_lat = lax.axis_index("lat") % 2
    odd_lon = lax.axis_index("lon") % 2
    partner_row = jnp.where(odd_lat == 1, 0, 2)
    rows = row // 2
    group = jnp.where(rows == 1, 0, jnp.where(rows == partner_row, 1, 2))
    west = lon < REACH
    east = lon >= 8 - REACH
    outer = jnp.where(odd_lon == 1, east, west)
    side = west | east
    center_slot = (row % 2) * 4 + lon - REACH
    side_slot = (row % 2) * 2 + jnp.where(west, lon, lon - 6)
    outer_phase = jnp.where(group == 1, 1, 2)
    outer_first = jnp.where(group == 0, 4, jnp.where(group == 1, 12, 8))
    inner_phase = jnp.where(group == 2, 4, group + 1)
    inner_first = jnp.where(group == 0, 8, 0)
    center_phase = jnp.where(group == 2, 3, group)
    phase = jnp.where(side, jnp.where(outer, outer_phase, inner_phase), center_phase)
    slot = jnp.where(
        side, jnp.where(outer, outer_first, inner_first) + side_slot, center_slot
    )
    live = jnp.arange(SLOTS, dtype=jnp.int32) < count
    phase = jnp.where(live, phase, PHASES)
    padding = jnp.arange(LIST - SLOTS, dtype=jnp.int32)
    entries = jnp.concatenate(
        [own + slot * 16 + (taper + 8) % 16 * 1024, jnp.full((LIST - SLOTS,), 8, jnp.int32)]
    )
    phases = jnp.concatenate([phase, jnp.minimum(padding // (3 * UNROLL), PHASES)])
    index = jnp.arange(LIST, dtype=jnp.int32)
    earlier = (phases[:, None] == phases[None, :]) & (index[:, None] < index[None, :])
    place = jnp.sum(earlier.astype(jnp.int32), axis=0)
    return entries + (phases * LIST + place) * 16384


def pairs_of(lists, phase, home, window_anom, window_innov, tapers, total, even, odd):
    def entry_at(group, lane):
        return lists[phase * LIST + group * UNROLL + lane]

    def tiles(group, kept):
        for lane in range(UNROLL):
            entry = entry_at(group, lane)
            product = lax.dot_general(
                window_anom[(entry >> 4) & 63],
                home[entry & 7],
                (((0,), (0,)), ((), ())),
                preferred_element_type=F32,
            )
            kept[lane] = (product * tapers[(entry >> 10) & 15].astype(F32)).astype(BF16)

    def increments(group, kept):
        for lane in range(UNROLL):
            entry = entry_at(group, lane)
            total[entry & 15] += jnp.dot(
                window_innov[(entry >> 4) & 63], kept[lane], preferred_element_type=F32
            )

    def two_groups(step, carry):
        tiles(2 * step + 1, odd)
        increments(2 * step, even)
        tiles(2 * step + 2, even)
        increments(2 * step + 1, odd)
        return carry

    tiles(0, even)
    groups = (lists[COUNTS + phase] + UNROLL - 1) // UNROLL
    lax.fori_loop(0, (groups + 1) // 2, two_groups, 0)


def side_kernel(anom, innov, after, *rest):
    *sides, done = rest
    first = 2 * (lax.axis_index("lon") % 2)
    copies = []
    for place, side in zip((2 - first, first), sides):
        for part, value in ((0, anom), (1, innov)):
            copies.append(
                pltpu.make_async_copy(
                    value.at[:, pl.ds(place, REACH)], side.at[part], done.at[len(copies)]
                )
            )
    for copy in copies:
        copy.start()
    for copy in copies:
        copy.wait()


def first_kernel(entries, *refs):
    sources, (total, lists, even, odd, home, innov, tapers, done) = (refs[:3], refs[3:])
    copies = [
        pltpu.make_async_copy(source, target, done.at[i])
        for i, (source, target) in enumerate(zip(sources, (home, innov, tapers)))
    ]
    for copy in copies:
        copy.start()

    def place(step, carry):
        for lane in range(8):
            entry = entries[step * 8 + lane]
            lists[entry >> 14] = entry & 16383
        return carry

    lax.fori_loop(0, LIST // 8, place, 0)
    for phase in range(PHASES):
        first = entries[SLOTS + 3 * UNROLL * phase] >> 14
        lists[COUNTS + phase] = first - phase * LIST
    total[...] = jnp.zeros_like(total)
    for copy in copies:
        copy.wait()
    pairs_of(lists, 0, home, home, innov, tapers, total, even, odd)


def gathered(parts, sides, anom, innov):
    first = 0
    if parts is not None:
        anom[0:8] = parts[0][...]
        innov[0:8] = parts[1][...]
        first = 8
    for side in sides:
        anom[first : first + 4] = side[0]
        innov[first : first + 4] = side[1]
        first += 4


def middle_kernel(phase, centers, lists, home, tapers, *rest):
    parts, (total, anom, innov, even, odd) = (rest[:-5], rest[-5:])
    gathered(parts[:2] if centers else None, parts[2:] if centers else parts, anom, innov)
    total[...] = jnp.zeros_like(total)
    pairs_of(lists, phase, home, anom, innov, tapers, total, even, odd)


def last_kernel(lists, home, tapers, side, *rest):
    before, (out, total, anom, innov, even, odd) = (rest[:-6], rest[-6:])
    gathered(None, (side,), anom, innov)
    total[...] = jnp.zeros_like(total)
    pairs_of(lists, 4, home, anom, innov, tapers, total, even, odd)
    for own in range(8):
        prior = home[own].astype(F32)
        increment = total[own]
        for part in before:
            increment += part[own]
        posterior = prior - increment * (1.0 / (MEMBERS - 1))
        prior_spread = jnp.sqrt(jnp.sum(prior * prior, axis=0, keepdims=True) / (MEMBERS - 1))
        posterior_spread = jnp.sqrt(
            jnp.sum(posterior * posterior, axis=0, keepdims=True) / (MEMBERS - 1) + 1e-06
        )
        out[own] = posterior * (0.7 * prior_spread / posterior_spread + 0.3)


HBM = pl.BlockSpec(memory_space=pltpu.HBM)
ANY = pl.BlockSpec(memory_space=pl.ANY)
SMEM = pl.BlockSpec(memory_space=pltpu.SMEM)
VMEM = pl.BlockSpec(memory_space=pltpu.VMEM)
TOTAL = jax.ShapeDtypeStruct((9, MEMBERS, BLOCK), F32)
SIDE = jax.ShapeDtypeStruct((2, 2, REACH, MEMBERS, BLOCK), BF16)


def called(kernel, name, specs, out_shape, out_specs, scratch, pairs):
    return pl.pallas_call(
        kernel,
        in_specs=specs,
        out_shape=out_shape,
        out_specs=out_specs,
        scratch_shapes=scratch,
        compiler_params=pltpu.CompilerParams(vmem_limit_bytes=VMEM_LIMIT),
        cost_estimate=pl.CostEstimate(
            flops=pairs * 16 * MEMBERS * BLOCK * BLOCK, bytes_accessed=4 * 2**20, transcendentals=0
        ),
        name=name,
    )


def local(
    anomalies, innovations, taper_table, pair_own, pair_window, pair_taper, pair_owner, pair_count
):
    def flat(value):
        return value.reshape(8, MEMBERS, BLOCK)

    def flat_side(value):
        return value.reshape(2, 4, MEMBERS, BLOCK)

    def sides_of(anom, innov, after, count):
        return called(
            side_kernel,
            "sides",
            [ANY] * 3,
            (SIDE,) * count,
            (ANY,) * count,
            [pltpu.SemaphoreType.DMA((2 * count,))],
            0,
        )(anom, innov, after)

    partner = [permuted(v, to_partner) for v in (anomalies, innovations)]
    entries = slot_entries(
        pair_own.reshape(-1),
        pair_window.reshape(-1),
        pair_taper.reshape(-1),
        pair_count.reshape(()),
    )
    inner, outer = sides_of(anomalies, innovations, entries, 2)
    partner_outer = permuted(outer, to_diagonal)
    home_inner = permuted(inner, to_other_core)
    beyond_outer = permuted(outer, to_far_diagonal)
    beyond = [permuted(v, to_beyond) for v in partner]
    inner, outer = sides_of(*partner, entries, 2)
    home_outer = permuted(outer, to_diagonal)
    partner_inner = permuted(inner, to_other_core)

    home = flat(anomalies)
    held = [pltpu.VMEM((UNROLL, BLOCK, BLOCK), BF16)] * 2
    scratch = lambda count: [pltpu.VMEM((count, MEMBERS, BLOCK), BF16)] * 2 + held

    total, lists = called(
        first_kernel,
        "home_pairs",
        [SMEM, HBM, HBM, HBM],
        (TOTAL, jax.ShapeDtypeStruct((COUNTS + PHASES,), jnp.int32)),
        (VMEM, SMEM),
        held
        + [pltpu.VMEM((8, MEMBERS, BLOCK), BF16)] * 2
        + [pltpu.VMEM(taper_table.shape, BF16), pltpu.SemaphoreType.DMA((3,))],
        56,
    )(entries, home, flat(innovations), taper_table)
    def more(phase, name, pairs, centers, sides):
        parts = [flat(v) for v in centers] + [flat_side(v) for v in sides]
        return called(
            functools.partial(middle_kernel, phase, bool(centers)),
            name,
            [SMEM] + [VMEM] * (2 + len(parts)),
            TOTAL,
            VMEM,
            scratch(4 * len(centers) + 4 * len(sides)),
            pairs,
        )(lists, home, taper_table, *parts)

    totals = [total]
    totals.append(more(1, "partner_pairs", 63, partner, [home_inner, partner_outer]))
    totals.append(more(2, "side_pairs", 30, [], [partner_inner, home_outer, beyond_outer]))
    beyond_inner = permuted(sides_of(*beyond, totals[2], 1)[0], to_other_core)
    totals.append(more(3, "beyond_pairs", 42, beyond, []))
    out = called(
        last_kernel,
        "inflation",
        [SMEM] + [VMEM] * 7,
        jax.ShapeDtypeStruct((8, MEMBERS, BLOCK), F32),
        VMEM,
        [pltpu.VMEM(TOTAL.shape, F32)] + scratch(4),
        9,
    )(lists, home, taper_table, flat_side(beyond_inner), *totals)
    return out.reshape(anomalies.shape)


def solution(mesh):
    placed = (
        P("lat", "lon", None, None),
        P("lat", "lon", None, None),
        P(),
        P("lat", "lon", None),
        P("lat", "lon", None),
        P("lat", "lon", None),
        P("lat", "lon", None),
        P("lat", "lon"),
    )
    return jax.shard_map(
        local, mesh=mesh, in_specs=placed, out_specs=P("lat", "lon", None, None), check_vma=False
    )
```

time: 54.4 us -> 49.9 us (0.917)
  the two profiles are of different devices: /device:TPU:225 before, /device:TPU:33 now
where the time goes in v2:
time: 49.9 us; the launch traced here: 49.4 us
  Pallas kernels  24.8 us (50%)
  starting transfers between devices  17.8 us (36%)
  local copies, waits for them, and re-layouts  3.5 us (7%)
  other arithmetic  2.39 us (5%)
  between operations  0.82 us (2%)
    ppermute x10, starting transfers between devices, permuted(): return lax.ppermute(value, ('lat', 'lon'), pairs)  17.8 us
    pallas_call x3, Pallas kernels, more(): called(functools.partial(middle_kernel, phase, bool(centers)), name, [SME...  13.9 us
    pallas_call x1, Pallas kernels, local(): called(first_kernel, 'home_pairs', [SMEM, HBM, HBM, HBM], (TOTAL, jax.Sha...  6.63 us
    unnamed x10, local copies, waits for them, and re-layouts  3.5 us
    pallas_call x1, Pallas kernels, local(): called(last_kernel, 'inflation', [SMEM] + [VMEM] * 7, jax.ShapeDtypeStruc...  3.39 us
  transfers between devices with their start and end apart: 10, of which 0 were waited for; matrix products, arithmetic and copies ran while one was open for 5% of the time, Pallas kernels for 43%

profile of v2, /device:TPU:33, one launch (start us, length us, event | category | flops | bytes accessed | tf_op | source)
XLA Modules:
  0.0 49.4 jit_solution(3532381892821934329)
XLA Ops:
  0.0 1.2 %collective-permute-start = (bf16[2,4,64,256]{3,2,1,0:T(8,128)(2,1)}, bf16[2,4,64,256]{3,2,1,0:T(8,128)(2,1)S(1)}, u32[]{:S(2)}, u32[]{:S(2)}) collective-permute-start(bf16[2,4,64,256]{3,2,1,0:T(8,128)(2,1)} %anom.1), channel_id=1, source_target_pairs={{0,16},{1,17},{2,18},{3,19},{4,20},{5,21},{6,22},{7,23},{8,24},{9,... | collective-permute-start | bytes 786440 | tf_op jit(solution)/shard_map/ppermute | solution.py:30
  1.2 0.3 collective-permute-start.2
  2.1 0.7 %broadcast_add_fusion = s32[1,1,200]{2,1,0:T(1,128)S(1)} fusion(s32[1,1,200]{2,1,0:T(1,128)} %param.13), kind=kLoop, calls=%fused_computation.38 | loop fusion | flops 200 | bytes 1600 | tf_op jit(solution)/shard_map/add | solution.py:83
  2.8 0.7 %fusion.5 = (s32[200]{0:T(256)S(1)}, s32[200]{0:T(256)S(1)}) fusion(s32[200]{0:T(256)S(1)} %bitcast.34, s32[200]{0:T(256)} %bitcast.37, pred[]{:T(512)S(6)} %eq.48, s32[200]{0:T(256)} %bitcast.35, s32[]{:T(128)S(6)} %select_n.107), kind=kLoop, calls=%fused_computation.29 | loop fusion | flops 15200 | bytes 4005 | tf_op jit(solution)/shard_map/add | solution.py:83
  3.6 0.7 %compare_select_fusion.4 = s32[200]{0:T(256)S(1)} fusion(s32[200]{0:T(256)S(1)} %get-tuple-element.18, s32[]{:T(128)} %bitcast.17, pred[]{:T(512)S(6)} %eq.48, s32[200]{0:T(256)} %bitcast.36), kind=kLoop, calls=%fused_computation.10 | loop fusion | flops 5000 | bytes 2405 | tf_op jit(solution)/shard_map/jit(_where)/select_n | solution.py:80
  4.2 0.1 pad_add_fusion
  4.3 0.1 convert_reduce_fusion
  4.5 0.1 multiply_add_fusion.entries.after
  4.5 0.0 copy-start.2
  4.5 1.0 %copy-done.2 = bf16[2,4,64,256]{3,2,1,0:T(8,128)(2,1)S(1)} copy-done((bf16[2,4,64,256]{3,2,1,0:T(8,128)(2,1)S(1)}, bf16[2,4,64,256]{3,2,1,0:T(8,128)(2,1)}, u32[]{:S(2)}) %copy-start.2) | copy-done | bytes 262168
  5.5 0.0 copy-start.4
  5.5 0.9 %copy-done.4 = bf16[2,4,64,256]{3,2,1,0:T(8,128)(2,1)S(1)} copy-done((bf16[2,4,64,256]{3,2,1,0:T(8,128)(2,1)S(1)}, bf16[2,4,64,256]{3,2,1,0:T(8,128)(2,1)}, u32[]{:S(2)}) %copy-start.4) | copy-done | bytes 262168
  6.4 0.4 sides.4
  6.8 3.7 %collective-permute-start.9 = (bf16[2,2,2,64,256]{4,3,2,1,0:T(8,128)(2,1)S(1)}, bf16[2,2,2,64,256]{4,3,2,1,0:T(8,128)(2,1)S(1)}, u32[]{:S(2)}, u32[]{:S(2)}) collective-permute-start(bf16[2,2,2,64,256]{4,3,2,1,0:T(8,128)(2,1)S(1)} %get-tuple-element.14), channel_id=1, source_target_pairs={{0,31},{1,18},{2,17},{3,20},{4,19},{5,22},{6,21},{7,24},{8,23},{9,... | collective-permute-start | bytes 786440 | tf_op jit(solution)/shard_map/ppermute | solution.py:30
  10.5 0.0 collective-permute-start.6
  10.5 4.0 %collective-permute-start.8 = (bf16[2,2,2,64,256]{4,3,2,1,0:T(8,128)(2,1)S(1)}, bf16[2,2,2,64,256]{4,3,2,1,0:T(8,128)(2,1)S(1)}, u32[]{:S(2)}, u32[]{:S(2)}) collective-permute-start(bf16[2,2,2,64,256]{4,3,2,1,0:T(8,128)(2,1)S(1)} %get-tuple-element.16), channel_id=1, source_target_pairs={{0,1},{1,0},{2,3},{3,2},{4,5},{5,4},{6,7},{7,6},{8,9},{9,8},{10,11... | collective-permute-start | bytes 786440 | tf_op jit(solution)/shard_map/ppermute | solution.py:30
  14.5 0.0 copy-start
  14.5 1.6 %copy-done = bf16[16,256,256]{2,1,0:T(8,128)(2,1)S(1)} copy-done((bf16[16,256,256]{2,1,0:T(8,128)(2,1)S(1)}, bf16[16,256,256]{2,1,0:T(8,128)(2,1)}, u32[]{:S(2)}) %copy-start) | copy-done | bytes 2097176
  16.1 0.0 copy-start.1
  16.1 0.0 copy-start.3
  16.1 6.6 %home_pairs.1 = (f32[9,64,256]{2,1,0:T(8,128)S(1)}, s32[1589]{0:T(1024)S(1)}) custom-call(s32[264]{0:T(512)S(1)} %multiply_add_fusion.entries.after, bf16[8,64,256]{2,1,0:T(8,128)(2,1)S(1)} %bitcast.18, bf16[8,64,256]{2,1,0:T(8,128)(2,1)S(1)} %bitcast.23, bf16[16,256,256]{2,1,0:T(8,128)(2,1)S(1)} %copy-done), custom_call_target="tpu_custom_call" | custom-call | flops 3758096384 | bytes 4194304 | tf_op jit(solution)/shard_map/home_pairs/pallas_call | solution.py:268
  22.7 0.0 collective-permute-done.anom
  22.7 0.0 collective-permute-done.2.innov
  22.7 0.4 sides.3
  23.1 0.1 collective-permute-start.4
  23.2 0.1 collective-permute-start.5
  23.3 0.0 collective-permute-done.8
  23.3 1.8 %collective-permute-start.1 = (bf16[2,4,64,256]{3,2,1,0:T(8,128)(2,1)S(1)}, bf16[2,4,64,256]{3,2,1,0:T(8,128)(2,1)S(1)}, u32[]{:S(2)}, u32[]{:S(2)}) collective-permute-start(bf16[2,4,64,256]{3,2,1,0:T(8,128)(2,1)S(1)} %collective-permute-done.anom), channel_id=1, source_target_pairs={{0,32},{1,33},{2,34},{3,35},{4,36},{5,37},{6,38},{7,39},{8,40},{9,... | collective-permute-start | bytes 786440 | tf_op jit(solution)/shard_map/ppermute | solution.py:30
  25.1 0.0 collective-permute-done.9
  25.1 2.2 %collective-permute-start.3 = (bf16[2,4,64,256]{3,2,1,0:T(8,128)(2,1)S(1)}, bf16[2,4,64,256]{3,2,1,0:T(8,128)(2,1)S(1)}, u32[]{:S(2)}, u32[]{:S(2)}) collective-permute-start(bf16[2,4,64,256]{3,2,1,0:T(8,128)(2,1)S(1)} %collective-permute-done.2.innov), channel_id=1, source_target_pairs={{0,32},{1,33},{2,34},{3,35},{4,36},{5,37},{6,38},{7,39},{8,40},{9,... | collective-permute-start | bytes 786440 | tf_op jit(solution)/shard_map/ppermute | solution.py:30
  27.4 0.0 copy-done.1
  27.4 0.0 copy-done.3
  27.4 5.5 %partner_pairs.1.rest_1_ = f32[9,64,256]{2,1,0:T(8,128)S(1)} custom-call(s32[1589]{0:T(1024)S(1)} %get-tuple-element.11.lists, bf16[8,64,256]{2,1,0:T(8,128)(2,1)S(1)} %bitcast.19, bf16[16,256,256]{2,1,0:T(8,128)(2,1)S(1)} %copy-done.1, bf16[8,64,256]{2,1,0:T(8,128)(2,1)S(1)} %bitcast.24, bf16[8,64,256]{2,1,0:T(8,128)(2,1)S(1)} %bitcast.25, ...), custom_call_target="tpu_custom_call" | custom-call | flops 4227858432 | bytes 4194304 | tf_op jit(solution)/shard_map/partner_pairs/pallas_call | solution.py:281
  32.8 0.0 collective-permute-done.6
  32.9 0.0 collective-permute-done.4
  32.9 0.0 collective-permute-done.5
  32.9 3.6 %side_pairs.1.after.rest_2_ = f32[9,64,256]{2,1,0:T(8,128)S(1)} custom-call(s32[1589]{0:T(1024)S(1)} %get-tuple-element.11.lists, bf16[8,64,256]{2,1,0:T(8,128)(2,1)S(1)} %bitcast.20, bf16[16,256,256]{2,1,0:T(8,128)(2,1)S(1)} %copy-done.1, bf16[2,4,64,256]{3,2,1,0:T(8,128)(2,1)S(1)} %bitcast.32, bf16[2,4,64,256]{3,2,1,0:T(8,128)(2,1)S(1)} %bitcast.33, ...), custom_call_target="tpu_custom_call" | custom-call | flops 2013265920 | bytes 4194304 | tf_op jit(solution)/shard_map/side_pairs/pallas_call | solution.py:281
  36.5 0.0 collective-permute-done.1.anom
  36.5 0.0 collective-permute-done.3.innov
  36.5 0.2 sides.5
  36.7 4.5 %collective-permute-start.7 = (bf16[2,2,2,64,256]{4,3,2,1,0:T(8,128)(2,1)S(1)}, bf16[2,2,2,64,256]{4,3,2,1,0:T(8,128)(2,1)S(1)}, u32[]{:S(2)}, u32[]{:S(2)}) collective-permute-start(bf16[2,2,2,64,256]{4,3,2,1,0:T(8,128)(2,1)S(1)} %sides.5), channel_id=1, source_target_pairs={{0,1},{1,0},{2,3},{3,2},{4,5},{5,4},{6,7},{7,6},{8,9},{9,8},{10,11... | collective-permute-start | bytes 786440 | tf_op jit(solution)/shard_map/ppermute | solution.py:30
  41.1 4.8 %beyond_pairs.1.rest_3_ = f32[9,64,256]{2,1,0:T(8,128)S(1)} custom-call(s32[1589]{0:T(1024)S(1)} %get-tuple-element.11.lists, bf16[8,64,256]{2,1,0:T(8,128)(2,1)S(1)} %bitcast.21, bf16[16,256,256]{2,1,0:T(8,128)(2,1)S(1)} %copy-done.1, bf16[8,64,256]{2,1,0:T(8,128)(2,1)S(1)} %bitcast.26, bf16[8,64,256]{2,1,0:T(8,128)(2,1)S(1)} %bitcast.27), custom_call_target="tpu_custom_call" | custom-call | flops 2818572288 | bytes 4194304 | tf_op jit(solution)/shard_map/beyond_pairs/pallas_call | solution.py:281
  46.0 0.0 collective-permute-done.7
  46.0 3.4 %inflation.1 = f32[8,64,256]{2,1,0:T(8,128)} custom-call(s32[1589]{0:T(1024)S(1)} %get-tuple-element.11.lists, bf16[8,64,256]{2,1,0:T(8,128)(2,1)S(1)} %bitcast.22, bf16[16,256,256]{2,1,0:T(8,128)(2,1)S(1)} %copy-done.1, bf16[2,4,64,256]{3,2,1,0:T(8,128)(2,1)S(1)} %bitcast.28, f32[9,64,256]{2,1,0:T(8,128)S(1)} %get-tuple-element.15.rest_0_, ...), custom_call_target="tpu_custom_call" | custom-call | flops 603979776 | bytes 4194304 | tf_op jit(solution)/shard_map/inflation/pallas_call | solution.py:296
  (1 shorter events, 0.0 us)
Async XLA Ops:
  0.0 22.7 %collective-permute-start = (bf16[2,4,64,256]{3,2,1,0:T(8,128)(2,1)}, bf16[2,4,64,256]{3,2,1,0:T(8,128)(2,1)S(1)}, u32[]{:S(2)}, u32[]{:S(2)}) collective-permute-start(bf16[2,4,64,256]{3,2,1,0:T(8,128)(2,1)} %anom.1), channel_id=1, source_target_pairs={{0,16},{1,17},{2,18},{3,19},{4,20},{5,21},{6,22},{7,23},{8,24},{9,... | collective-permute-start | bytes 786440 | tf_op jit(solution)/shard_map/ppermute | solution.py:30
  1.2 21.5 %collective-permute-start.2 = (bf16[2,4,64,256]{3,2,1,0:T(8,128)(2,1)}, bf16[2,4,64,256]{3,2,1,0:T(8,128)(2,1)S(1)}, u32[]{:S(2)}, u32[]{:S(2)}) collective-permute-start(bf16[2,4,64,256]{3,2,1,0:T(8,128)(2,1)} %innov.1), channel_id=1, source_target_pairs={{0,16},{1,17},{2,18},{3,19},{4,20},{5,21},{6,22},{7,23},{8,24},{9,... | collective-permute-start | bytes 786440 | tf_op jit(solution)/shard_map/ppermute | solution.py:30
  4.5 1.0 %copy-start.2 = (bf16[2,4,64,256]{3,2,1,0:T(8,128)(2,1)S(1)}, bf16[2,4,64,256]{3,2,1,0:T(8,128)(2,1)}, u32[]{:S(2)}) copy-start(bf16[2,4,64,256]{3,2,1,0:T(8,128)(2,1)} %anom.1) | copy-start | bytes 786436
  5.5 0.9 %copy-start.4 = (bf16[2,4,64,256]{3,2,1,0:T(8,128)(2,1)S(1)}, bf16[2,4,64,256]{3,2,1,0:T(8,128)(2,1)}, u32[]{:S(2)}) copy-start(bf16[2,4,64,256]{3,2,1,0:T(8,128)(2,1)} %innov.1) | copy-start | bytes 786436
  6.8 18.3 %collective-permute-start.9 = (bf16[2,2,2,64,256]{4,3,2,1,0:T(8,128)(2,1)S(1)}, bf16[2,2,2,64,256]{4,3,2,1,0:T(8,128)(2,1)S(1)}, u32[]{:S(2)}, u32[]{:S(2)}) collective-permute-start(bf16[2,2,2,64,256]{4,3,2,1,0:T(8,128)(2,1)S(1)} %get-tuple-element.14), channel_id=1, source_target_pairs={{0,31},{1,18},{2,17},{3,20},{4,19},{5,22},{6,21},{7,24},{8,23},{9,... | collective-permute-start | bytes 786440 | tf_op jit(solution)/shard_map/ppermute | solution.py:30
  10.5 22.3 %collective-permute-start.6 = (bf16[2,2,2,64,256]{4,3,2,1,0:T(8,128)(2,1)S(1)}, bf16[2,2,2,64,256]{4,3,2,1,0:T(8,128)(2,1)S(1)}, u32[]{:S(2)}, u32[]{:S(2)}) collective-permute-start(bf16[2,2,2,64,256]{4,3,2,1,0:T(8,128)(2,1)S(1)} %get-tuple-element.14), channel_id=1, source_target_pairs={{0,15},{1,2},{2,1},{3,4},{4,3},{5,6},{6,5},{7,8},{8,7},{9,10},{10,... | collective-permute-start | bytes 786440 | tf_op jit(solution)/shard_map/ppermute | solution.py:30
  10.5 12.8 %collective-permute-start.8 = (bf16[2,2,2,64,256]{4,3,2,1,0:T(8,128)(2,1)S(1)}, bf16[2,2,2,64,256]{4,3,2,1,0:T(8,128)(2,1)S(1)}, u32[]{:S(2)}, u32[]{:S(2)}) collective-permute-start(bf16[2,2,2,64,256]{4,3,2,1,0:T(8,128)(2,1)S(1)} %get-tuple-element.16), channel_id=1, source_target_pairs={{0,1},{1,0},{2,3},{3,2},{4,5},{5,4},{6,7},{7,6},{8,9},{9,8},{10,11... | collective-permute-start | bytes 786440 | tf_op jit(solution)/shard_map/ppermute | solution.py:30
  14.5 1.6 %copy-start = (bf16[16,256,256]{2,1,0:T(8,128)(2,1)S(1)}, bf16[16,256,256]{2,1,0:T(8,128)(2,1)}, u32[]{:S(2)}) copy-start(bf16[16,256,256]{2,1,0:T(8,128)(2,1)} %tapers.7) | copy-start | bytes 6291460
  16.1 11.3 %copy-start.1 = (bf16[16,256,256]{2,1,0:T(8,128)(2,1)S(1)}, bf16[16,256,256]{2,1,0:T(8,128)(2,1)}, u32[]{:S(2)}) copy-start(bf16[16,256,256]{2,1,0:T(8,128)(2,1)} %tapers.7) | copy-start | bytes 6291460
  16.1 11.3 %copy-start.3 = (bf16[2,4,64,256]{3,2,1,0:T(8,128)(2,1)S(1)}, bf16[2,4,64,256]{3,2,1,0:T(8,128)(2,1)}, u32[]{:S(2)}) copy-start(bf16[2,4,64,256]{3,2,1,0:T(8,128)(2,1)} %anom.1) | copy-start | bytes 786436
  23.1 9.7 %collective-permute-start.4 = (bf16[2,2,2,64,256]{4,3,2,1,0:T(8,128)(2,1)S(1)}, bf16[2,2,2,64,256]{4,3,2,1,0:T(8,128)(2,1)S(1)}, u32[]{:S(2)}, u32[]{:S(2)}) collective-permute-start(bf16[2,2,2,64,256]{4,3,2,1,0:T(8,128)(2,1)S(1)} %get-tuple-element.12), channel_id=1, source_target_pairs={{0,1},{1,0},{2,3},{3,2},{4,5},{5,4},{6,7},{7,6},{8,9},{9,8},{10,11... | collective-permute-start | bytes 786440 | tf_op jit(solution)/shard_map/ppermute | solution.py:30
  23.2 9.6 %collective-permute-start.5 = (bf16[2,2,2,64,256]{4,3,2,1,0:T(8,128)(2,1)S(1)}, bf16[2,2,2,64,256]{4,3,2,1,0:T(8,128)(2,1)S(1)}, u32[]{:S(2)}, u32[]{:S(2)}) collective-permute-start(bf16[2,2,2,64,256]{4,3,2,1,0:T(8,128)(2,1)S(1)} %get-tuple-element.13), channel_id=1, source_target_pairs={{0,31},{1,18},{2,17},{3,20},{4,19},{5,22},{6,21},{7,24},{8,23},{9,... | collective-permute-start | bytes 786440 | tf_op jit(solution)/shard_map/ppermute | solution.py:30
  23.3 13.1 %collective-permute-start.1 = (bf16[2,4,64,256]{3,2,1,0:T(8,128)(2,1)S(1)}, bf16[2,4,64,256]{3,2,1,0:T(8,128)(2,1)S(1)}, u32[]{:S(2)}, u32[]{:S(2)}) collective-permute-start(bf16[2,4,64,256]{3,2,1,0:T(8,128)(2,1)S(1)} %collective-permute-done.anom), channel_id=1, source_target_pairs={{0,32},{1,33},{2,34},{3,35},{4,36},{5,37},{6,38},{7,39},{8,40},{9,... | collective-permute-start | bytes 786440 | tf_op jit(solution)/shard_map/ppermute | solution.py:30
  25.1 11.4 %collective-permute-start.3 = (bf16[2,4,64,256]{3,2,1,0:T(8,128)(2,1)S(1)}, bf16[2,4,64,256]{3,2,1,0:T(8,128)(2,1)S(1)}, u32[]{:S(2)}, u32[]{:S(2)}) collective-permute-start(bf16[2,4,64,256]{3,2,1,0:T(8,128)(2,1)S(1)} %collective-permute-done.2.innov), channel_id=1, source_target_pairs={{0,32},{1,33},{2,34},{3,35},{4,36},{5,37},{6,38},{7,39},{8,40},{9,... | collective-permute-start | bytes 786440 | tf_op jit(solution)/shard_map/ppermute | solution.py:30
  36.7 9.3 %collective-permute-start.7 = (bf16[2,2,2,64,256]{4,3,2,1,0:T(8,128)(2,1)S(1)}, bf16[2,2,2,64,256]{4,3,2,1,0:T(8,128)(2,1)S(1)}, u32[]{:S(2)}, u32[]{:S(2)}) collective-permute-start(bf16[2,2,2,64,256]{4,3,2,1,0:T(8,128)(2,1)S(1)} %sides.5), channel_id=1, source_target_pairs={{0,1},{1,0},{2,3},{3,2},{4,5},{5,4},{6,7},{7,6},{8,9},{9,8},{10,11... | collective-permute-start | bytes 786440 | tf_op jit(solution)/shard_map/ppermute | solution.py:30

commit v3 on v2

v3 whole, which is shorter than its diff:
```python
import functools

import jax
import jax.numpy as jnp
from jax import lax
from jax.experimental import pallas as pl
from jax.experimental.pallas import tpu as pltpu
from jax.sharding import PartitionSpec as P

MEMBERS = 64
BLOCK = 256
REACH = 2
UNROLL = 4
LIST = 264
SLOTS = 200
PHASES = 3
COUNTS = (PHASES + 1) * LIST
VMEM_LIMIT = 8 * 2**20
F32 = jnp.float32
BF16 = jnp.bfloat16


def permuted(value, target):
    bands, lons = (lax.axis_size("lat"), lax.axis_size("lon"))
    pairs = []
    for i in range(bands):
        for j in range(lons):
            a, b = target(i, j)
            pairs.append((i * lons + j, a * lons + b % lons))
    return lax.ppermute(value, ("lat", "lon"), pairs)


def to_partner(i, j):
    return (i ^ 1, j)


def to_beyond(i, j):
    last = lax.axis_size("lat") - 1
    target = i + 2 if i % 2 == 0 else i - 2
    return (target if 0 <= target <= last else i ^ 1, j)


def to_far_diagonal(i, j):
    last = lax.axis_size("lat") - 1
    target = i + 1 if i % 2 else i - 1
    return (target if 0 <= target <= last else i, j + 1 if j % 2 else j - 1)


def to_diagonal(i, j):
    return (i ^ 1, j + 1 if j % 2 else j - 1)


def to_other_core(i, j):
    return (i, j ^ 1)


def slot_entries(own, window, taper, count):
    row, lon = (window // 8, window % 8)
    odd_lat = lax.axis_index("lat") % 2
    odd_lon = lax.axis_index("lon") % 2
    partner_row = jnp.where(odd_lat == 1, 0, 2)
    rows = row // 2
    group = jnp.where(rows == 1, 0, jnp.where(rows == partner_row, 1, 2))
    west = lon < REACH
    east = lon >= 8 - REACH
    outer = jnp.where(odd_lon == 1, east, west)
    side = west | east
    center_slot = jnp.where(group == 1, 8, 0) + (row % 2) * 4 + lon - REACH
    side_slot = (row % 2) * 2 + jnp.where(west, lon, lon - 6)
    late = ~outer | (group == 0)
    phase = jnp.where(side, jnp.where(late, 2, 1), group // 2)
    outer_slot = jnp.where(group == 1, 8, 12)
    slot = jnp.where(side, jnp.where(outer, outer_slot, group * 4) + side_slot, center_slot)
    live = jnp.arange(SLOTS, dtype=jnp.int32) < count
    phase = jnp.where(live, phase, PHASES)
    padding = jnp.arange(LIST - SLOTS, dtype=jnp.int32)
    entries = jnp.concatenate(
        [own + slot * 16 + (taper + 8) % 16 * 1024, jnp.full((LIST - SLOTS,), 8, jnp.int32)]
    )
    phases = jnp.concatenate([phase, jnp.minimum(padding // (3 * UNROLL), PHASES)])
    index = jnp.arange(LIST, dtype=jnp.int32)
    earlier = (phases[:, None] == phases[None, :]) & (index[:, None] < index[None, :])
    place = jnp.sum(earlier.astype(jnp.int32), axis=0)
    return entries + (phases * LIST + place) * 16384


def pairs_of(lists, phase, home, window_anom, window_innov, tapers, total, even, odd):
    def entry_at(group, lane):
        return lists[phase * LIST + group * UNROLL + lane]

    def tiles(group, kept):
        for lane in range(UNROLL):
            entry = entry_at(group, lane)
            product = lax.dot_general(
                window_anom[(entry >> 4) & 63],
                home[entry & 7],
                (((0,), (0,)), ((), ())),
                preferred_element_type=F32,
            )
            kept[lane] = (product * tapers[(entry >> 10) & 15].astype(F32)).astype(BF16)

    def increments(group, kept):
        for lane in range(UNROLL):
            entry = entry_at(group, lane)
            total[entry & 15] += jnp.dot(
                window_innov[(entry >> 4) & 63], kept[lane], preferred_element_type=F32
            )

    def two_groups(step, carry):
        tiles(2 * step + 1, odd)
        increments(2 * step, even)
        tiles(2 * step + 2, even)
        increments(2 * step + 1, odd)
        return carry

    tiles(0, even)
    groups = (lists[COUNTS + phase] + UNROLL - 1) // UNROLL
    lax.fori_loop(0, (groups + 1) // 2, two_groups, 0)


def copied(pairs, done):
    copies = [
        pltpu.make_async_copy(source, target, done.at[i])
        for i, (source, target) in enumerate(pairs)
    ]
    for copy in copies:
        copy.start()
    for copy in copies:
        copy.wait()


def load_kernel(anom, innov, table, after, home, home_innov, tapers, outer, done):
    columns = pl.ds(2 * (lax.axis_index("lon") % 2), REACH)
    pairs = [(anom, home), (innov, home_innov)]
    pairs += [(v.at[:, columns], outer.at[i]) for i, v in enumerate((anom, innov))]
    pairs += [(table.at[4 * i : 4 * i + 4], tapers.at[4 * i : 4 * i + 4]) for i in range(4)]
    copied(pairs, done)


def outer_kernel(anom, innov, side, done):
    columns = pl.ds(2 * (lax.axis_index("lon") % 2), REACH)
    copied([(v.at[:, columns], side.at[i]) for i, v in enumerate((anom, innov))], done)


def inner_kernel(near, anom, innov, *refs):
    side, done = refs[-2:]
    columns = pl.ds(2 - 2 * (lax.axis_index("lon") % 2), REACH)
    pairs = [(near.at[i], side.at[i, 0:4]) for i in range(2)]
    pairs += [(v.at[:, columns], side.at[i, 4:6]) for i, v in enumerate((anom, innov))]
    copied(pairs, done)


def near_kernel(entries, home, home_innov, tapers, partner, partner_innov, *refs):
    total, lists, near, anom, innov, even, odd = refs
    anom[0:8] = home[...]
    anom[8:16] = partner[...]
    innov[0:8] = home_innov[...]
    innov[8:16] = partner_innov[...]
    first = 2 - 2 * (lax.axis_index("lon") % 2)
    for row in range(4):
        near[0, row] = anom[pl.ds(row * 4 + first, REACH)]
        near[1, row] = innov[pl.ds(row * 4 + first, REACH)]

    def place(step, carry):
        for lane in range(8):
            entry = entries[step * 8 + lane]
            lists[entry >> 14] = entry & 16383
        return carry

    lax.fori_loop(0, LIST // 8, place, 0)
    for phase in range(PHASES):
        first = entries[SLOTS + 3 * UNROLL * phase] >> 14
        lists[COUNTS + phase] = first - phase * LIST
    total[...] = jnp.zeros_like(total)
    pairs_of(lists, 0, anom, anom, innov, tapers, total, even, odd)


def gathered(centers, sides, anom, innov):
    anom[0:8] = centers[0][...]
    innov[0:8] = centers[1][...]
    for i, side in enumerate(sides):
        anom[8 + 4 * i : 12 + 4 * i] = side[0]
        innov[8 + 4 * i : 12 + 4 * i] = side[1]


def middle_kernel(phase, lists, home, tapers, *rest):
    parts, (total, anom, innov, even, odd) = (rest[:-5], rest[-5:])
    gathered(parts[:2], parts[2:], anom, innov)
    total[...] = jnp.zeros_like(total)
    pairs_of(lists, phase, home, anom, innov, tapers, total, even, odd)


def last_kernel(lists, home, tapers, inner, outer, *rest):
    before, (out, total, anom, innov, even, odd) = (rest[:-6], rest[-6:])
    for part, blocks in enumerate((anom, innov)):
        blocks[0:12] = inner[part]
        blocks[12:16] = outer[part]
    total[...] = jnp.zeros_like(total)
    pairs_of(lists, 2, home, anom, innov, tapers, total, even, odd)
    for own in range(8):
        prior = home[own].astype(F32)
        increment = total[own]
        for part in before:
            increment += part[own]
        posterior = prior - increment * (1.0 / (MEMBERS - 1))
        prior_spread = jnp.sqrt(jnp.sum(prior * prior, axis=0, keepdims=True) / (MEMBERS - 1))
        posterior_spread = jnp.sqrt(
            jnp.sum(posterior * posterior, axis=0, keepdims=True) / (MEMBERS - 1) + 1e-06
        )
        out[own] = posterior * (0.7 * prior_spread / posterior_spread + 0.3)


ANY = pl.BlockSpec(memory_space=pl.ANY)
SMEM = pl.BlockSpec(memory_space=pltpu.SMEM)
VMEM = pl.BlockSpec(memory_space=pltpu.VMEM)
TOTAL = jax.ShapeDtypeStruct((9, MEMBERS, BLOCK), F32)


def called(kernel, name, specs, out_shape, out_specs, scratch, pairs):
    return pl.pallas_call(
        kernel,
        in_specs=specs,
        out_shape=out_shape,
        out_specs=out_specs,
        scratch_shapes=scratch,
        compiler_params=pltpu.CompilerParams(vmem_limit_bytes=VMEM_LIMIT),
        cost_estimate=pl.CostEstimate(
            flops=pairs * 16 * MEMBERS * BLOCK * BLOCK, bytes_accessed=4 * 2**20, transcendentals=0
        ),
        name=name,
    )


def local(
    anomalies, innovations, taper_table, pair_own, pair_window, pair_taper, pair_owner, pair_count
):
    def flat(value):
        return value.reshape(8, MEMBERS, BLOCK)

    def flat_side(value):
        return value.reshape(2, -1, MEMBERS, BLOCK)

    partner = [permuted(v, to_partner) for v in (anomalies, innovations)]
    entries = slot_entries(
        pair_own.reshape(-1),
        pair_window.reshape(-1),
        pair_taper.reshape(-1),
        pair_count.reshape(()),
    )
    row = jax.ShapeDtypeStruct(anomalies.shape, BF16)
    anomalies, innovations, taper_table, outer = called(
        load_kernel,
        "load",
        [ANY] * 4,
        (
            row,
            row,
            jax.ShapeDtypeStruct(taper_table.shape, BF16),
            jax.ShapeDtypeStruct((2, 2, REACH, MEMBERS, BLOCK), BF16),
        ),
        (VMEM,) * 4,
        [pltpu.SemaphoreType.DMA((8,))],
        0,
    )(anomalies, innovations, taper_table, entries)
    partner_outer = permuted(outer, to_diagonal)
    beyond_outer = permuted(outer, to_far_diagonal)
    beyond = [permuted(v, to_beyond) for v in partner]
    partner_cut = called(
        outer_kernel,
        "outer_sides",
        [ANY] * 2,
        jax.ShapeDtypeStruct(outer.shape, BF16),
        ANY,
        [pltpu.SemaphoreType.DMA((2,))],
        0,
    )(*partner)
    home_outer = permuted(partner_cut, to_diagonal)
    home = flat(anomalies)
    held = [pltpu.VMEM((UNROLL, BLOCK, BLOCK), BF16)] * 2

    def blocks(count):
        return [pltpu.VMEM((count, MEMBERS, BLOCK), BF16)] * 2 + held

    near_total, lists, near = called(
        near_kernel,
        "near_pairs",
        [SMEM] + [VMEM] * 5,
        (
            TOTAL,
            jax.ShapeDtypeStruct((COUNTS + PHASES,), jnp.int32),
            jax.ShapeDtypeStruct((2, 4, REACH, MEMBERS, BLOCK), BF16),
        ),
        (VMEM, SMEM, VMEM),
        blocks(16),
        98,
    )(entries, home, flat(innovations), taper_table, flat(partner[0]), flat(partner[1]))
    inner = permuted(
        called(
            inner_kernel,
            "inner_sides",
            [ANY] * 6,
            jax.ShapeDtypeStruct((2, 6, REACH, MEMBERS, BLOCK), BF16),
            ANY,
            [pltpu.SemaphoreType.DMA((4,))],
            0,
        )(near, *beyond, home_outer, partner_outer, beyond_outer),
        to_other_core,
    )
    beyond_total = called(
        functools.partial(middle_kernel, 1),
        "beyond_pairs",
        [SMEM] + [VMEM] * 6,
        TOTAL,
        VMEM,
        blocks(16),
        60,
    )(
        lists,
        home,
        taper_table,
        flat(beyond[0]),
        flat(beyond[1]),
        flat_side(partner_outer),
        flat_side(beyond_outer),
    )
    totals = [near_total, beyond_total]
    out = called(
        last_kernel,
        "inflation",
        [SMEM] + [VMEM] * 6,
        jax.ShapeDtypeStruct((8, MEMBERS, BLOCK), F32),
        VMEM,
        [pltpu.VMEM(TOTAL.shape, F32)] + [pltpu.VMEM((16, MEMBERS, BLOCK), BF16)] * 2 + held,
        42,
    )(lists, home, taper_table, flat_side(inner), flat_side(home_outer), *totals)
    return out.reshape(anomalies.shape)


def solution(mesh):
    placed = (
        P("lat", "lon", None, None),
        P("lat", "lon", None, None),
        P(),
        P("lat", "lon", None),
        P("lat", "lon", None),
        P("lat", "lon", None),
        P("lat", "lon", None),
        P("lat", "lon"),
    )
    return jax.shard_map(
        local, mesh=mesh, in_specs=placed, out_specs=P("lat", "lon", None, None), check_vma=False
    )
```

time: 49.9 us -> 46.5 us (0.932)
  the two profiles are of different devices: /device:TPU:33 before, /device:TPU:225 now
where the time goes in v3:
time: 46.5 us; the launch traced here: 46.3 us
  Pallas kernels  23.2 us (50%)
  starting transfers between devices  13.2 us (28%)
  local copies, waits for them, and re-layouts  3.49 us (8%)
  waiting for transfers between devices  3.2 us (7%)
  other arithmetic  2.4 us (5%)
  between operations  0.75 us (2%)
    ppermute x8, starting transfers between devices, permuted(): return lax.ppermute(value, ('lat', 'lon'), pairs)  13.2 us
    pallas_call x1, Pallas kernels, local(): called(near_kernel, 'near_pairs', [SMEM] + [VMEM] * 5, (TOTAL, jax.ShapeD...  10.3 us
    pallas_call x1, Pallas kernels, local(): called(functools.partial(middle_kernel, 1), 'beyond_pairs', [SMEM] + [VME...  6.14 us
    pallas_call x1, Pallas kernels, local(): called(last_kernel, 'inflation', [SMEM] + [VMEM] * 6, jax.ShapeDtypeStruc...  5.9 us
    unnamed x6, local copies, waits for them, and re-layouts  3.49 us
    ppermute x8, waiting for transfers between devices, permuted(): return lax.ppermute(value, ('lat', 'lon'), pairs)  3.2 us
  transfers between devices with their start and end apart: 8, of which 2 were waited for; matrix products, arithmetic and copies ran while one was open for 5% of the time, Pallas kernels for 37%

profile of v3, /device:TPU:225, one launch (start us, length us, event | category | flops | bytes accessed | tf_op | source)
XLA Modules:
  0.0 46.3 jit_solution(17239185585857342036)
XLA Ops:
  0.0 1.2 %collective-permute-start = (bf16[2,4,64,256]{3,2,1,0:T(8,128)(2,1)}, bf16[2,4,64,256]{3,2,1,0:T(8,128)(2,1)S(1)}, u32[]{:S(2)}, u32[]{:S(2)}) collective-permute-start(bf16[2,4,64,256]{3,2,1,0:T(8,128)(2,1)} %anom.1), channel_id=1, source_target_pairs={{0,16},{1,17},{2,18},{3,19},{4,20},{5,21},{6,22},{7,23},{8,24},{9,... | collective-permute-start | bytes 786440 | tf_op jit(solution)/shard_map/ppermute | solution.py:30
  1.2 0.3 collective-permute-start.1
  2.1 0.7 %broadcast_add_fusion = s32[1,1,200]{2,1,0:T(1,128)S(1)} fusion(s32[1,1,200]{2,1,0:T(1,128)} %param.13), kind=kLoop, calls=%fused_computation.37 | loop fusion | flops 200 | bytes 1600 | tf_op jit(solution)/shard_map/add | solution.py:78
  2.8 0.7 %fusion.5 = (s32[200]{0:T(256)S(1)}, s32[200]{0:T(256)S(1)}) fusion(s32[200]{0:T(256)S(1)} %bitcast.28, s32[200]{0:T(256)} %bitcast.31, pred[]{:T(512)S(6)} %eq.44, s32[200]{0:T(256)} %bitcast.29, s32[]{:T(128)S(6)} %select_n.98), kind=kLoop, calls=%fused_computation.29 | loop fusion | flops 15200 | bytes 4005 | tf_op jit(solution)/shard_map/add | solution.py:78
  3.6 0.7 %compare_select_fusion.2 = s32[200]{0:T(256)S(1)} fusion(s32[200]{0:T(256)S(1)} %get-tuple-element.20, s32[]{:T(128)} %bitcast.15, pred[]{:T(512)S(6)} %eq.44, s32[200]{0:T(256)} %bitcast.30), kind=kLoop, calls=%fused_computation.10 | loop fusion | flops 6000 | bytes 2405 | tf_op jit(solution)/shard_map/jit(_where)/select_n | solution.py:75
  4.3 0.1 pad_add_fusion
  4.3 0.1 convert_reduce_fusion
  4.5 0.1 multiply_add_fusion.after.entries
  4.5 0.0 copy-start
  4.5 1.6 %copy-done = bf16[16,256,256]{2,1,0:T(8,128)(2,1)S(1)} copy-done((bf16[16,256,256]{2,1,0:T(8,128)(2,1)S(1)}, bf16[16,256,256]{2,1,0:T(8,128)(2,1)}, u32[]{:S(2)}) %copy-start) | copy-done | bytes 2097176
  6.1 0.0 copy-start.1
  6.1 0.9 %copy-done.1 = bf16[2,4,64,256]{3,2,1,0:T(8,128)(2,1)S(1)} copy-done((bf16[2,4,64,256]{3,2,1,0:T(8,128)(2,1)S(1)}, bf16[2,4,64,256]{3,2,1,0:T(8,128)(2,1)}, u32[]{:S(2)}) %copy-start.1) | copy-done | bytes 262168
  7.1 0.0 copy-start.2
  7.1 0.9 %copy-done.2 = bf16[2,4,64,256]{3,2,1,0:T(8,128)(2,1)S(1)} copy-done((bf16[2,4,64,256]{3,2,1,0:T(8,128)(2,1)S(1)}, bf16[2,4,64,256]{3,2,1,0:T(8,128)(2,1)}, u32[]{:S(2)}) %copy-start.2) | copy-done | bytes 262168
  8.0 0.4 load.1
  8.5 4.2 %collective-permute-start.6 = (bf16[2,2,2,64,256]{4,3,2,1,0:T(8,128)(2,1)S(1)}, bf16[2,2,2,64,256]{4,3,2,1,0:T(8,128)(2,1)S(1)}, u32[]{:S(2)}, u32[]{:S(2)}) collective-permute-start(bf16[2,2,2,64,256]{4,3,2,1,0:T(8,128)(2,1)S(1)} %get-tuple-element.17), channel_id=1, source_target_pairs={{0,15},{1,2},{2,1},{3,4},{4,3},{5,6},{6,5},{7,8},{8,7},{9,10},{10,... | collective-permute-start | bytes 786440 | tf_op jit(solution)/shard_map/ppermute | solution.py:30
  12.6 0.0 collective-permute-start.5
  12.6 0.0 collective-permute-done.anom
  12.6 0.4 collective-permute-done.1.innov
  13.0 0.2 outer_sides.1
  13.2 4.0 %collective-permute-start.4 = (bf16[2,2,2,64,256]{4,3,2,1,0:T(8,128)(2,1)S(1)}, bf16[2,2,2,64,256]{4,3,2,1,0:T(8,128)(2,1)S(1)}, u32[]{:S(2)}, u32[]{:S(2)}) collective-permute-start(bf16[2,2,2,64,256]{4,3,2,1,0:T(8,128)(2,1)S(1)} %outer_sides.1), channel_id=1, source_target_pairs={{0,31},{1,18},{2,17},{3,20},{4,19},{5,22},{6,21},{7,24},{8,23},{9,... | collective-permute-start | bytes 786440 | tf_op jit(solution)/shard_map/ppermute | solution.py:30
  17.2 0.1 collective-permute-start.2
  17.2 0.6 %collective-permute-start.3 = (bf16[2,4,64,256]{3,2,1,0:T(8,128)(2,1)S(1)}, bf16[2,4,64,256]{3,2,1,0:T(8,128)(2,1)S(1)}, u32[]{:S(2)}, u32[]{:S(2)}) collective-permute-start(bf16[2,4,64,256]{3,2,1,0:T(8,128)(2,1)S(1)} %collective-permute-done.1.innov), channel_id=1, source_target_pairs={{0,32},{1,33},{2,34},{3,35},{4,36},{5,37},{6,38},{7,39},{8,40},{9,... | collective-permute-start | bytes 786440 | tf_op jit(solution)/shard_map/ppermute | solution.py:30
  17.9 10.3 %near_pairs.1 = (f32[9,64,256]{2,1,0:T(8,128)S(1)}, s32[1059]{0:T(1024)S(1)}, bf16[2,4,2,64,256]{4,3,2,1,0:T(8,128)(2,1)S(1)}) custom-call(s32[264]{0:T(512)S(1)} %multiply_add_fusion.after.entries, bf16[8,64,256]{2,1,0:T(8,128)(2,1)S(1)} %bitcast.24, bf16[8,64,256]{2,1,0:T(8,128)(2,1)S(1)} %bitcast.27, bf16[16,256,256]{2,1,0:T(8,128)(2,1)S(1)} %get-tuple-element.14.tapers, ...), custom_call_target="tpu_custom_call" | custom-call | flops 6576668672 | bytes 4194304 | tf_op jit(solution)/shard_map/near_pairs/pallas_call | solution.py:284
  28.2 0.0 collective-permute-done.6.refs_2_
  28.2 0.0 collective-permute-done.5.refs_1_
  28.2 0.0 collective-permute-done.2.anom
  28.2 2.8 %collective-permute-done.4.refs_0_ = bf16[2,2,2,64,256]{4,3,2,1,0:T(8,128)(2,1)S(1)} collective-permute-done((bf16[2,2,2,64,256]{4,3,2,1,0:T(8,128)(2,1)S(1)}, bf16[2,2,2,64,256]{4,3,2,1,0:T(8,128)(2,1)S(1)}, u32[]{:S(2)}, u32[]{:S(2)}) %collective-permute-start.4) | collective-permute-done | bytes 262176 | tf_op jit(solution)/shard_map/ppermute | solution.py:30
  31.0 0.0 collective-permute-done.3.innov
  31.0 0.2 inner_sides.1
  31.3 2.9 %collective-permute-start.7 = (bf16[2,6,2,64,256]{4,3,2,1,0:T(8,128)(2,1)S(1)}, bf16[2,6,2,64,256]{4,3,2,1,0:T(8,128)(2,1)S(1)}, u32[]{:S(2)}, u32[]{:S(2)}) collective-permute-start(bf16[2,6,2,64,256]{4,3,2,1,0:T(8,128)(2,1)S(1)} %inner_sides.1), channel_id=1, source_target_pairs={{0,1},{1,0},{2,3},{3,2},{4,5},{5,4},{6,7},{7,6},{8,9},{9,8},{10,11... | collective-permute-start | bytes 2359304 | tf_op jit(solution)/shard_map/ppermute | solution.py:30
  34.2 6.1 %beyond_pairs.1.rest_1_ = f32[9,64,256]{2,1,0:T(8,128)S(1)} custom-call(s32[1059]{0:T(1024)S(1)} %get-tuple-element.15.lists, bf16[8,64,256]{2,1,0:T(8,128)(2,1)S(1)} %bitcast.25, bf16[16,256,256]{2,1,0:T(8,128)(2,1)S(1)} %get-tuple-element.14.tapers, bf16[8,64,256]{2,1,0:T(8,128)(2,1)S(1)} %bitcast.21, bf16[8,64,256]{2,1,0:T(8,128)(2,1)S(1)} %bitcast.22, ...), custom_call_target="tpu_custom_call" | custom-call | flops 4026531840 | bytes 4194304 | tf_op jit(solution)/shard_map/beyond_pairs/pallas_call | solution.py:309
  40.3 0.0 collective-permute-done.7
  40.4 5.9 %inflation.1 = f32[8,64,256]{2,1,0:T(8,128)} custom-call(s32[1059]{0:T(1024)S(1)} %get-tuple-element.15.lists, bf16[8,64,256]{2,1,0:T(8,128)(2,1)S(1)} %bitcast.26, bf16[16,256,256]{2,1,0:T(8,128)(2,1)S(1)} %get-tuple-element.14.tapers, bf16[2,12,64,256]{3,2,1,0:T(8,128)(2,1)S(1)} %bitcast.23, bf16[2,4,64,256]{3,2,1,0:T(8,128)(2,1)S(1)} %bitcast.20, ...), custom_call_target="tpu_custom_call" | custom-call | flops 2818572288 | bytes 4194304 | tf_op jit(solution)/shard_map/inflation/pallas_call | solution.py:327
  (1 shorter events, 0.0 us)
Async XLA Ops:
  0.0 12.6 %collective-permute-start = (bf16[2,4,64,256]{3,2,1,0:T(8,128)(2,1)}, bf16[2,4,64,256]{3,2,1,0:T(8,128)(2,1)S(1)}, u32[]{:S(2)}, u32[]{:S(2)}) collective-permute-start(bf16[2,4,64,256]{3,2,1,0:T(8,128)(2,1)} %anom.1), channel_id=1, source_target_pairs={{0,16},{1,17},{2,18},{3,19},{4,20},{5,21},{6,22},{7,23},{8,24},{9,... | collective-permute-start | bytes 786440 | tf_op jit(solution)/shard_map/ppermute | solution.py:30
  1.2 11.8 %collective-permute-start.1 = (bf16[2,4,64,256]{3,2,1,0:T(8,128)(2,1)}, bf16[2,4,64,256]{3,2,1,0:T(8,128)(2,1)S(1)}, u32[]{:S(2)}, u32[]{:S(2)}) collective-permute-start(bf16[2,4,64,256]{3,2,1,0:T(8,128)(2,1)} %innov.1), channel_id=1, source_target_pairs={{0,16},{1,17},{2,18},{3,19},{4,20},{5,21},{6,22},{7,23},{8,24},{9,... | collective-permute-start | bytes 786440 | tf_op jit(solution)/shard_map/ppermute | solution.py:30
  4.5 1.6 %copy-start = (bf16[16,256,256]{2,1,0:T(8,128)(2,1)S(1)}, bf16[16,256,256]{2,1,0:T(8,128)(2,1)}, u32[]{:S(2)}) copy-start(bf16[16,256,256]{2,1,0:T(8,128)(2,1)} %table.1) | copy-start | bytes 6291460
  6.1 0.9 %copy-start.1 = (bf16[2,4,64,256]{3,2,1,0:T(8,128)(2,1)S(1)}, bf16[2,4,64,256]{3,2,1,0:T(8,128)(2,1)}, u32[]{:S(2)}) copy-start(bf16[2,4,64,256]{3,2,1,0:T(8,128)(2,1)} %anom.1) | copy-start | bytes 786436
  7.1 0.9 %copy-start.2 = (bf16[2,4,64,256]{3,2,1,0:T(8,128)(2,1)S(1)}, bf16[2,4,64,256]{3,2,1,0:T(8,128)(2,1)}, u32[]{:S(2)}) copy-start(bf16[2,4,64,256]{3,2,1,0:T(8,128)(2,1)} %innov.1) | copy-start | bytes 786436
  8.5 19.7 %collective-permute-start.6 = (bf16[2,2,2,64,256]{4,3,2,1,0:T(8,128)(2,1)S(1)}, bf16[2,2,2,64,256]{4,3,2,1,0:T(8,128)(2,1)S(1)}, u32[]{:S(2)}, u32[]{:S(2)}) collective-permute-start(bf16[2,2,2,64,256]{4,3,2,1,0:T(8,128)(2,1)S(1)} %get-tuple-element.17), channel_id=1, source_target_pairs={{0,15},{1,2},{2,1},{3,4},{4,3},{5,6},{6,5},{7,8},{8,7},{9,10},{10,... | collective-permute-start | bytes 786440 | tf_op jit(solution)/shard_map/ppermute | solution.py:30
  12.6 15.6 %collective-permute-start.5 = (bf16[2,2,2,64,256]{4,3,2,1,0:T(8,128)(2,1)S(1)}, bf16[2,2,2,64,256]{4,3,2,1,0:T(8,128)(2,1)S(1)}, u32[]{:S(2)}, u32[]{:S(2)}) collective-permute-start(bf16[2,2,2,64,256]{4,3,2,1,0:T(8,128)(2,1)S(1)} %get-tuple-element.17), channel_id=1, source_target_pairs={{0,31},{1,18},{2,17},{3,20},{4,19},{5,22},{6,21},{7,24},{8,23},{9,... | collective-permute-start | bytes 786440 | tf_op jit(solution)/shard_map/ppermute | solution.py:30
  13.2 17.8 %collective-permute-start.4 = (bf16[2,2,2,64,256]{4,3,2,1,0:T(8,128)(2,1)S(1)}, bf16[2,2,2,64,256]{4,3,2,1,0:T(8,128)(2,1)S(1)}, u32[]{:S(2)}, u32[]{:S(2)}) collective-permute-start(bf16[2,2,2,64,256]{4,3,2,1,0:T(8,128)(2,1)S(1)} %outer_sides.1), channel_id=1, source_target_pairs={{0,31},{1,18},{2,17},{3,20},{4,19},{5,22},{6,21},{7,24},{8,23},{9,... | collective-permute-start | bytes 786440 | tf_op jit(solution)/shard_map/ppermute | solution.py:30
  17.2 11.0 %collective-permute-start.2 = (bf16[2,4,64,256]{3,2,1,0:T(8,128)(2,1)S(1)}, bf16[2,4,64,256]{3,2,1,0:T(8,128)(2,1)S(1)}, u32[]{:S(2)}, u32[]{:S(2)}) collective-permute-start(bf16[2,4,64,256]{3,2,1,0:T(8,128)(2,1)S(1)} %collective-permute-done.anom), channel_id=1, source_target_pairs={{0,32},{1,33},{2,34},{3,35},{4,36},{5,37},{6,38},{7,39},{8,40},{9,... | collective-permute-start | bytes 786440 | tf_op jit(solution)/shard_map/ppermute | solution.py:30
  17.2 13.8 %collective-permute-start.3 = (bf16[2,4,64,256]{3,2,1,0:T(8,128)(2,1)S(1)}, bf16[2,4,64,256]{3,2,1,0:T(8,128)(2,1)S(1)}, u32[]{:S(2)}, u32[]{:S(2)}) collective-permute-start(bf16[2,4,64,256]{3,2,1,0:T(8,128)(2,1)S(1)} %collective-permute-done.1.innov), channel_id=1, source_target_pairs={{0,32},{1,33},{2,34},{3,35},{4,36},{5,37},{6,38},{7,39},{8,40},{9,... | collective-permute-start | bytes 786440 | tf_op jit(solution)/shard_map/ppermute | solution.py:30
  31.3 9.1 %collective-permute-start.7 = (bf16[2,6,2,64,256]{4,3,2,1,0:T(8,128)(2,1)S(1)}, bf16[2,6,2,64,256]{4,3,2,1,0:T(8,128)(2,1)S(1)}, u32[]{:S(2)}, u32[]{:S(2)}) collective-permute-start(bf16[2,6,2,64,256]{4,3,2,1,0:T(8,128)(2,1)S(1)} %inner_sides.1), channel_id=1, source_target_pairs={{0,1},{1,0},{2,3},{3,2},{4,5},{5,4},{6,7},{7,6},{8,9},{9,8},{10,11... | collective-permute-start | bytes 2359304 | tf_op jit(solution)/shard_map/ppermute | solution.py:30

commit v4 on v3

--- a/solution.py
+++ b/solution.py
@@ -67,9 +67,8 @@
     side = west | east
     center_slot = jnp.where(group == 1, 8, 0) + (row % 2) * 4 + lon - REACH
     side_slot = (row % 2) * 2 + jnp.where(west, lon, lon - 6)
-    late = ~outer | (group == 0)
-    phase = jnp.where(side, jnp.where(late, 2, 1), group // 2)
-    outer_slot = jnp.where(group == 1, 8, 12)
+    phase = jnp.where(side, jnp.where(outer, 1, 2), group // 2)
+    outer_slot = jnp.where(group == 1, 8, jnp.where(group == 2, 12, 16))
     slot = jnp.where(side, jnp.where(outer, outer_slot, group * 4) + side_slot, center_slot)
     live = jnp.arange(SLOTS, dtype=jnp.int32) < count
     phase = jnp.where(live, phase, PHASES)
@@ -190,11 +189,10 @@
     pairs_of(lists, phase, home, anom, innov, tapers, total, even, odd)
 
 
-def last_kernel(lists, home, tapers, inner, outer, *rest):
+def last_kernel(lists, home, tapers, inner, *rest):
     before, (out, total, anom, innov, even, odd) = (rest[:-6], rest[-6:])
     for part, blocks in enumerate((anom, innov)):
         blocks[0:12] = inner[part]
-        blocks[12:16] = outer[part]
     total[...] = jnp.zeros_like(total)
     pairs_of(lists, 2, home, anom, innov, tapers, total, even, odd)
     for own in range(8):
@@ -309,11 +307,11 @@
     beyond_total = called(
         functools.partial(middle_kernel, 1),
         "beyond_pairs",
-        [SMEM] + [VMEM] * 6,
+        [SMEM] + [VMEM] * 7,
         TOTAL,
         VMEM,
-        blocks(16),
-        60,
+        blocks(20),
+        72,
     )(
         lists,
         home,
@@ -322,17 +320,18 @@
         flat(beyond[1]),
         flat_side(partner_outer),
         flat_side(beyond_outer),
+        flat_side(home_outer),
     )
     totals = [near_total, beyond_total]
     out = called(
         last_kernel,
         "inflation",
-        [SMEM] + [VMEM] * 6,
+        [SMEM] + [VMEM] * 5,
         jax.ShapeDtypeStruct((8, MEMBERS, BLOCK), F32),
         VMEM,
-        [pltpu.VMEM(TOTAL.shape, F32)] + [pltpu.VMEM((16, MEMBERS, BLOCK), BF16)] * 2 + held,
-        42,
-    )(lists, home, taper_table, flat_side(inner), flat_side(home_outer), *totals)
+        [pltpu.VMEM(TOTAL.shape, F32)] + [pltpu.VMEM((12, MEMBERS, BLOCK), BF16)] * 2 + held,
+        30,
+    )(lists, home, taper_table, flat_side(inner), *totals)
     return out.reshape(anomalies.shape)
 
 

time: 46.5 us -> 45.8 us (0.985)
  Pallas kernels: 23.2 us -> 22.5 us
    pallas_call x1, Pallas kernels: 5.9 us -> 4.61 us  [local(): called(last_kernel, 'inflation', [SMEM] + [VMEM] * 5, jax.ShapeDtypeStruc...]
    pallas_call x1, Pallas kernels: 6.14 us -> 6.77 us  [local(): called(functools.partial(middle_kernel, 1), 'beyond_pairs', [SMEM] + [VME...]
  transfers between devices with their start and end apart: 8 -> 8, of which waited for: 2 -> 2; matrix products, arithmetic and copies ran while one was open for 5% -> 5% of each run, Pallas kernels for 37% -> 39%
where the time goes in v4:
time: 45.8 us; the launch traced here: 45.6 us
  Pallas kernels  22.5 us (49%)
  starting transfers between devices  13.2 us (29%)
  local copies, waits for them, and re-layouts  3.49 us (8%)
  waiting for transfers between devices  3.2 us (7%)
  other arithmetic  2.4 us (5%)
  between operations  0.75 us (2%)
    ppermute x8, starting transfers between devices, permuted(): return lax.ppermute(value, ('lat', 'lon'), pairs)  13.2 us
    pallas_call x1, Pallas kernels, local(): called(near_kernel, 'near_pairs', [SMEM] + [VMEM] * 5, (TOTAL, jax.ShapeD...  10.3 us
    pallas_call x1, Pallas kernels, local(): called(functools.partial(middle_kernel, 1), 'beyond_pairs', [SMEM] + [VME...  6.77 us
    pallas_call x1, Pallas kernels, local(): called(last_kernel, 'inflation', [SMEM] + [VMEM] * 5, jax.ShapeDtypeStruc...  4.61 us
    unnamed x6, local copies, waits for them, and re-layouts  3.49 us
    ppermute x8, waiting for transfers between devices, permuted(): return lax.ppermute(value, ('lat', 'lon'), pairs)  3.2 us
  transfers between devices with their start and end apart: 8, of which 2 were waited for; matrix products, arithmetic and copies ran while one was open for 5% of the time, Pallas kernels for 39%

profile of v4, /device:TPU:225, one launch (start us, length us, event | category | flops | bytes accessed | tf_op | source)
XLA Modules:
  0.0 45.6 jit_solution(12614217774082960134)
XLA Ops:
  0.0 1.2 %collective-permute-start = (bf16[2,4,64,256]{3,2,1,0:T(8,128)(2,1)}, bf16[2,4,64,256]{3,2,1,0:T(8,128)(2,1)S(1)}, u32[]{:S(2)}, u32[]{:S(2)}) collective-permute-start(bf16[2,4,64,256]{3,2,1,0:T(8,128)(2,1)} %anom.1), channel_id=1, source_target_pairs={{0,16},{1,17},{2,18},{3,19},{4,20},{5,21},{6,22},{7,23},{8,24},{9,... | collective-permute-start | bytes 786440 | tf_op jit(solution)/shard_map/ppermute | solution.py:30
  1.2 0.3 collective-permute-start.1
  2.1 0.7 %broadcast_add_fusion = s32[1,1,200]{2,1,0:T(1,128)S(1)} fusion(s32[1,1,200]{2,1,0:T(1,128)} %param.13), kind=kLoop, calls=%fused_computation.39 | loop fusion | flops 200 | bytes 1600 | tf_op jit(solution)/shard_map/add | solution.py:77
  2.8 0.7 %fusion.7 = (s32[200]{0:T(256)S(1)}, s32[200]{0:T(256)S(1)}) fusion(s32[200]{0:T(256)S(1)} %bitcast.28, s32[200]{0:T(256)} %bitcast.31, pred[]{:T(512)S(6)} %eq.43, s32[200]{0:T(256)} %bitcast.29, s32[]{:T(128)S(6)} %select_n.102), kind=kLoop, calls=%fused_computation.31 | loop fusion | flops 15600 | bytes 4005 | tf_op jit(solution)/shard_map/add | solution.py:77
  3.6 0.7 %compare_select_fusion.2 = s32[200]{0:T(256)S(1)} fusion(s32[200]{0:T(256)S(1)} %get-tuple-element.20, s32[]{:T(128)} %bitcast.15, pred[]{:T(512)S(6)} %eq.43, s32[200]{0:T(256)} %bitcast.30), kind=kLoop, calls=%fused_computation.9 | loop fusion | flops 5400 | bytes 2405 | tf_op jit(solution)/shard_map/jit(_where)/select_n | solution.py:74
  4.2 0.1 pad_add_fusion
  4.3 0.1 convert_reduce_fusion
  4.5 0.1 multiply_add_fusion.after.entries
  4.5 0.0 copy-start
  4.5 1.6 %copy-done = bf16[16,256,256]{2,1,0:T(8,128)(2,1)S(1)} copy-done((bf16[16,256,256]{2,1,0:T(8,128)(2,1)S(1)}, bf16[16,256,256]{2,1,0:T(8,128)(2,1)}, u32[]{:S(2)}) %copy-start) | copy-done | bytes 2097176
  6.1 0.0 copy-start.1
  6.1 0.9 %copy-done.1 = bf16[2,4,64,256]{3,2,1,0:T(8,128)(2,1)S(1)} copy-done((bf16[2,4,64,256]{3,2,1,0:T(8,128)(2,1)S(1)}, bf16[2,4,64,256]{3,2,1,0:T(8,128)(2,1)}, u32[]{:S(2)}) %copy-start.1) | copy-done | bytes 262168
  7.1 0.0 copy-start.2
  7.1 0.9 %copy-done.2 = bf16[2,4,64,256]{3,2,1,0:T(8,128)(2,1)S(1)} copy-done((bf16[2,4,64,256]{3,2,1,0:T(8,128)(2,1)S(1)}, bf16[2,4,64,256]{3,2,1,0:T(8,128)(2,1)}, u32[]{:S(2)}) %copy-start.2) | copy-done | bytes 262168
  8.0 0.4 load.1
  8.5 4.2 %collective-permute-start.6 = (bf16[2,2,2,64,256]{4,3,2,1,0:T(8,128)(2,1)S(1)}, bf16[2,2,2,64,256]{4,3,2,1,0:T(8,128)(2,1)S(1)}, u32[]{:S(2)}, u32[]{:S(2)}) collective-permute-start(bf16[2,2,2,64,256]{4,3,2,1,0:T(8,128)(2,1)S(1)} %get-tuple-element.17), channel_id=1, source_target_pairs={{0,15},{1,2},{2,1},{3,4},{4,3},{5,6},{6,5},{7,8},{8,7},{9,10},{10,... | collective-permute-start | bytes 786440 | tf_op jit(solution)/shard_map/ppermute | solution.py:30
  12.6 0.0 collective-permute-start.5
  12.6 0.0 collective-permute-done.anom
  12.6 0.4 collective-permute-done.1.innov
  13.0 0.2 outer_sides.1
  13.2 4.0 %collective-permute-start.4 = (bf16[2,2,2,64,256]{4,3,2,1,0:T(8,128)(2,1)S(1)}, bf16[2,2,2,64,256]{4,3,2,1,0:T(8,128)(2,1)S(1)}, u32[]{:S(2)}, u32[]{:S(2)}) collective-permute-start(bf16[2,2,2,64,256]{4,3,2,1,0:T(8,128)(2,1)S(1)} %outer_sides.1), channel_id=1, source_target_pairs={{0,31},{1,18},{2,17},{3,20},{4,19},{5,22},{6,21},{7,24},{8,23},{9,... | collective-permute-start | bytes 786440 | tf_op jit(solution)/shard_map/ppermute | solution.py:30
  17.2 0.1 collective-permute-start.2
  17.2 0.6 %collective-permute-start.3 = (bf16[2,4,64,256]{3,2,1,0:T(8,128)(2,1)S(1)}, bf16[2,4,64,256]{3,2,1,0:T(8,128)(2,1)S(1)}, u32[]{:S(2)}, u32[]{:S(2)}) collective-permute-start(bf16[2,4,64,256]{3,2,1,0:T(8,128)(2,1)S(1)} %collective-permute-done.1.innov), channel_id=1, source_target_pairs={{0,32},{1,33},{2,34},{3,35},{4,36},{5,37},{6,38},{7,39},{8,40},{9,... | collective-permute-start | bytes 786440 | tf_op jit(solution)/shard_map/ppermute | solution.py:30
  17.9 10.3 %near_pairs.1 = (f32[9,64,256]{2,1,0:T(8,128)S(1)}, s32[1059]{0:T(1024)S(1)}, bf16[2,4,2,64,256]{4,3,2,1,0:T(8,128)(2,1)S(1)}) custom-call(s32[264]{0:T(512)S(1)} %multiply_add_fusion.after.entries, bf16[8,64,256]{2,1,0:T(8,128)(2,1)S(1)} %bitcast.24, bf16[8,64,256]{2,1,0:T(8,128)(2,1)S(1)} %bitcast.27, bf16[16,256,256]{2,1,0:T(8,128)(2,1)S(1)} %get-tuple-element.14.tapers, ...), custom_call_target="tpu_custom_call" | custom-call | flops 6576668672 | bytes 4194304 | tf_op jit(solution)/shard_map/near_pairs/pallas_call | solution.py:282
  28.2 0.0 collective-permute-done.6.refs_2_
  28.2 0.0 collective-permute-done.5.refs_1_
  28.2 0.0 collective-permute-done.2.anom
  28.2 2.8 %collective-permute-done.4.refs_0_ = bf16[2,2,2,64,256]{4,3,2,1,0:T(8,128)(2,1)S(1)} collective-permute-done((bf16[2,2,2,64,256]{4,3,2,1,0:T(8,128)(2,1)S(1)}, bf16[2,2,2,64,256]{4,3,2,1,0:T(8,128)(2,1)S(1)}, u32[]{:S(2)}, u32[]{:S(2)}) %collective-permute-start.4) | collective-permute-done | bytes 262176 | tf_op jit(solution)/shard_map/ppermute | solution.py:30
  31.0 0.0 collective-permute-done.3.innov
  31.0 0.2 inner_sides.1
  31.3 2.9 %collective-permute-start.7 = (bf16[2,6,2,64,256]{4,3,2,1,0:T(8,128)(2,1)S(1)}, bf16[2,6,2,64,256]{4,3,2,1,0:T(8,128)(2,1)S(1)}, u32[]{:S(2)}, u32[]{:S(2)}) collective-permute-start(bf16[2,6,2,64,256]{4,3,2,1,0:T(8,128)(2,1)S(1)} %inner_sides.1), channel_id=1, source_target_pairs={{0,1},{1,0},{2,3},{3,2},{4,5},{5,4},{6,7},{7,6},{8,9},{9,8},{10,11... | collective-permute-start | bytes 2359304 | tf_op jit(solution)/shard_map/ppermute | solution.py:30
  34.2 6.8 %beyond_pairs.1.rest_1_ = f32[9,64,256]{2,1,0:T(8,128)S(1)} custom-call(s32[1059]{0:T(1024)S(1)} %get-tuple-element.15.lists, bf16[8,64,256]{2,1,0:T(8,128)(2,1)S(1)} %bitcast.25, bf16[16,256,256]{2,1,0:T(8,128)(2,1)S(1)} %get-tuple-element.14.tapers, bf16[8,64,256]{2,1,0:T(8,128)(2,1)S(1)} %bitcast.21, bf16[8,64,256]{2,1,0:T(8,128)(2,1)S(1)} %bitcast.22, ...), custom_call_target="tpu_custom_call" | custom-call | flops 4831838208 | bytes 4194304 | tf_op jit(solution)/shard_map/beyond_pairs/pallas_call | solution.py:307
  41.0 0.0 collective-permute-done.7
  41.0 4.6 %inflation.1 = f32[8,64,256]{2,1,0:T(8,128)} custom-call(s32[1059]{0:T(1024)S(1)} %get-tuple-element.15.lists, bf16[8,64,256]{2,1,0:T(8,128)(2,1)S(1)} %bitcast.26, bf16[16,256,256]{2,1,0:T(8,128)(2,1)S(1)} %get-tuple-element.14.tapers, bf16[2,12,64,256]{3,2,1,0:T(8,128)(2,1)S(1)} %bitcast.23, f32[9,64,256]{2,1,0:T(8,128)S(1)} %get-tuple-element.18.rest_0_, ...), custom_call_target="tpu_custom_call" | custom-call | flops 2013265920 | bytes 4194304 | tf_op jit(solution)/shard_map/inflation/pallas_call | solution.py:326
  (1 shorter events, 0.0 us)
Async XLA Ops:
  0.0 12.6 %collective-permute-start = (bf16[2,4,64,256]{3,2,1,0:T(8,128)(2,1)}, bf16[2,4,64,256]{3,2,1,0:T(8,128)(2,1)S(1)}, u32[]{:S(2)}, u32[]{:S(2)}) collective-permute-start(bf16[2,4,64,256]{3,2,1,0:T(8,128)(2,1)} %anom.1), channel_id=1, source_target_pairs={{0,16},{1,17},{2,18},{3,19},{4,20},{5,21},{6,22},{7,23},{8,24},{9,... | collective-permute-start | bytes 786440 | tf_op jit(solution)/shard_map/ppermute | solution.py:30
  1.2 11.8 %collective-permute-start.1 = (bf16[2,4,64,256]{3,2,1,0:T(8,128)(2,1)}, bf16[2,4,64,256]{3,2,1,0:T(8,128)(2,1)S(1)}, u32[]{:S(2)}, u32[]{:S(2)}) collective-permute-start(bf16[2,4,64,256]{3,2,1,0:T(8,128)(2,1)} %innov.1), channel_id=1, source_target_pairs={{0,16},{1,17},{2,18},{3,19},{4,20},{5,21},{6,22},{7,23},{8,24},{9,... | collective-permute-start | bytes 786440 | tf_op jit(solution)/shard_map/ppermute | solution.py:30
  4.5 1.6 %copy-start = (bf16[16,256,256]{2,1,0:T(8,128)(2,1)S(1)}, bf16[16,256,256]{2,1,0:T(8,128)(2,1)}, u32[]{:S(2)}) copy-start(bf16[16,256,256]{2,1,0:T(8,128)(2,1)} %table.1) | copy-start | bytes 6291460
  6.1 0.9 %copy-start.1 = (bf16[2,4,64,256]{3,2,1,0:T(8,128)(2,1)S(1)}, bf16[2,4,64,256]{3,2,1,0:T(8,128)(2,1)}, u32[]{:S(2)}) copy-start(bf16[2,4,64,256]{3,2,1,0:T(8,128)(2,1)} %anom.1) | copy-start | bytes 786436
  7.1 0.9 %copy-start.2 = (bf16[2,4,64,256]{3,2,1,0:T(8,128)(2,1)S(1)}, bf16[2,4,64,256]{3,2,1,0:T(8,128)(2,1)}, u32[]{:S(2)}) copy-start(bf16[2,4,64,256]{3,2,1,0:T(8,128)(2,1)} %innov.1) | copy-start | bytes 786436
  8.5 19.7 %collective-permute-start.6 = (bf16[2,2,2,64,256]{4,3,2,1,0:T(8,128)(2,1)S(1)}, bf16[2,2,2,64,256]{4,3,2,1,0:T(8,128)(2,1)S(1)}, u32[]{:S(2)}, u32[]{:S(2)}) collective-permute-start(bf16[2,2,2,64,256]{4,3,2,1,0:T(8,128)(2,1)S(1)} %get-tuple-element.17), channel_id=1, source_target_pairs={{0,15},{1,2},{2,1},{3,4},{4,3},{5,6},{6,5},{7,8},{8,7},{9,10},{10,... | collective-permute-start | bytes 786440 | tf_op jit(solution)/shard_map/ppermute | solution.py:30
  12.6 15.6 %collective-permute-start.5 = (bf16[2,2,2,64,256]{4,3,2,1,0:T(8,128)(2,1)S(1)}, bf16[2,2,2,64,256]{4,3,2,1,0:T(8,128)(2,1)S(1)}, u32[]{:S(2)}, u32[]{:S(2)}) collective-permute-start(bf16[2,2,2,64,256]{4,3,2,1,0:T(8,128)(2,1)S(1)} %get-tuple-element.17), channel_id=1, source_target_pairs={{0,31},{1,18},{2,17},{3,20},{4,19},{5,22},{6,21},{7,24},{8,23},{9,... | collective-permute-start | bytes 786440 | tf_op jit(solution)/shard_map/ppermute | solution.py:30
  13.2 17.8 %collective-permute-start.4 = (bf16[2,2,2,64,256]{4,3,2,1,0:T(8,128)(2,1)S(1)}, bf16[2,2,2,64,256]{4,3,2,1,0:T(8,128)(2,1)S(1)}, u32[]{:S(2)}, u32[]{:S(2)}) collective-permute-start(bf16[2,2,2,64,256]{4,3,2,1,0:T(8,128)(2,1)S(1)} %outer_sides.1), channel_id=1, source_target_pairs={{0,31},{1,18},{2,17},{3,20},{4,19},{5,22},{6,21},{7,24},{8,23},{9,... | collective-permute-start | bytes 786440 | tf_op jit(solution)/shard_map/ppermute | solution.py:30
  17.2 11.0 %collective-permute-start.2 = (bf16[2,4,64,256]{3,2,1,0:T(8,128)(2,1)S(1)}, bf16[2,4,64,256]{3,2,1,0:T(8,128)(2,1)S(1)}, u32[]{:S(2)}, u32[]{:S(2)}) collective-permute-start(bf16[2,4,64,256]{3,2,1,0:T(8,128)(2,1)S(1)} %collective-permute-done.anom), channel_id=1, source_target_pairs={{0,32},{1,33},{2,34},{3,35},{4,36},{5,37},{6,38},{7,39},{8,40},{9,... | collective-permute-start | bytes 786440 | tf_op jit(solution)/shard_map/ppermute | solution.py:30
  17.2 13.8 %collective-permute-start.3 = (bf16[2,4,64,256]{3,2,1,0:T(8,128)(2,1)S(1)}, bf16[2,4,64,256]{3,2,1,0:T(8,128)(2,1)S(1)}, u32[]{:S(2)}, u32[]{:S(2)}) collective-permute-start(bf16[2,4,64,256]{3,2,1,0:T(8,128)(2,1)S(1)} %collective-permute-done.1.innov), channel_id=1, source_target_pairs={{0,32},{1,33},{2,34},{3,35},{4,36},{5,37},{6,38},{7,39},{8,40},{9,... | collective-permute-start | bytes 786440 | tf_op jit(solution)/shard_map/ppermute | solution.py:30
  31.3 9.7 %collective-permute-start.7 = (bf16[2,6,2,64,256]{4,3,2,1,0:T(8,128)(2,1)S(1)}, bf16[2,6,2,64,256]{4,3,2,1,0:T(8,128)(2,1)S(1)}, u32[]{:S(2)}, u32[]{:S(2)}) collective-permute-start(bf16[2,6,2,64,256]{4,3,2,1,0:T(8,128)(2,1)S(1)} %inner_sides.1), channel_id=1, source_target_pairs={{0,1},{1,0},{2,3},{3,2},{4,5},{5,4},{6,7},{7,6},{8,9},{9,8},{10,11... | collective-permute-start | bytes 2359304 | tf_op jit(solution)/shard_map/ppermute | solution.py:30
